TPU v7x, 32 devices: a whole 2x2x4 slice. The times are simulated.
32 devices in a mesh: seq: 8 (over z, core), tp: 4 (over y, x).
Axes of the slice: x: 2, y: 2, z: 4, core: 2. Of those that a mesh axis runs over, the one named last changes fastest.
Arguments:
- inputs: bfloat16 [4096, 1536], P(('seq', 'tp')), may hold values from -6 to 6
- positions: int32 [4096], P(('seq', 'tp')), may hold values from 0 to 4095, as said below
- attn_gain: float32 [1536], replicated, may hold values from 0.25 to 1.75
- w_query: bfloat16 [1536, 1536], replicated, may hold values from -0.15625 to 0.15625
- w_key: bfloat16 [1536, 1536], replicated, may hold values from -0.15625 to 0.15625
- w_value: bfloat16 [1536, 1536], replicated, may hold values from -0.15625 to 0.15625
- w_out: bfloat16 [1536, 1536], replicated, may hold values from -0.75 to 0.75
- lambda_params: float32 [4, 64], replicated, may hold values from -0.5 to 0.5
- sub_gain: float32 [128], replicated, may hold values from 0.25 to 1.75
- ffn_gain: float32 [1536], replicated, may hold values from 0.25 to 1.75
- w_gate: bfloat16 [1536, 4096], P(None, 'tp'), may hold values from -0.15625 to 0.15625
- w_up: bfloat16 [1536, 4096], P(None, 'tp'), may hold values from -0.15625 to 0.15625
- w_down: bfloat16 [4096, 1536], P('tp'), may hold values from -0.1875 to 0.1875
- cotangent: bfloat16 [4096, 1536], P(('seq', 'tp')), may hold values from -8 to 8
Outputs:
- output: bfloat16 [4096, 1536], P(('seq', 'tp'))
- input_grad: float32 [4096, 1536], P(('seq', 'tp'))
- attn_gain_grad: float32 [1536], P(('seq', 'tp'))
- query_grad: float32 [1536, 1536], P(('seq', 'tp'))
- key_grad: float32 [1536, 1536], P(('seq', 'tp'))
- value_grad: float32 [1536, 1536], P(('seq', 'tp'))
- out_grad: float32 [1536, 1536], P(('seq', 'tp'))
- lambda_grads: float32 [4, 64], replicated
- sub_gain_grad: float32 [128], replicated
- ffn_gain_grad: float32 [1536], P(('seq', 'tp'))
- gate_grad: float32 [1536, 4096], P('seq', 'tp')
- up_grad: float32 [1536, 4096], P('seq', 'tp')
- down_grad: float32 [4096, 1536], P('tp', 'seq')
- lambda_total: float32 [], replicated
- lambda_norm: float32 [], replicated
Inputs may be any that keep to these rules, and one draw needn't show every extreme that they name: positions holds each of 0 to 4095 once; each aligned run of 64 rows holds consecutive positions in rising order.
All inputs are finite; a program needn't handle non-finite values.
Results may differ from a plain program's by a relative error of at most 0.033.
Values may be sent and summed in bfloat16 or wider, within the bound.
A program may use at most 448 MiB of HBM per device.

v0:
```python
import math

import jax
import jax.numpy as jnp
from jax import lax
from jax.sharding import PartitionSpec as P

H = 12
HALF = 64
VW = 128
HW = 1536


eps = 1e-05
lambda_init = 0.8 - 0.6 * math.exp(-3.3)
masked_score = -1e30


def rms_scale(values):
    return lax.rsqrt(jnp.mean(values * values, axis=-1, keepdims=True) + eps)


def rms_back(values, inv_rms, gain_vec, upstream):
    weighted = upstream * gain_vec
    inner_mean = jnp.mean(weighted * values, axis=-1, keepdims=True)
    return inv_rms * weighted - values * (inv_rms * inv_rms * inv_rms) * inner_mean


def block_scores(query_rows, key_rows):
    score_scale = HALF ** (-0.5)
    first_map = (
        jnp.einsum(
            "qhd,khd->hqk",
            query_rows[:, :, :HALF],
            key_rows[:, :, :HALF],
            preferred_element_type=jnp.float32,
        )
        * score_scale
    )
    second_map = (
        jnp.einsum(
            "qhd,khd->hqk",
            query_rows[:, :, HALF:],
            key_rows[:, :, HALF:],
            preferred_element_type=jnp.float32,
        )
        * score_scale
    )
    return (first_map, second_map)


def online(running_max, row_total, weighted, scores, allowed, value_rows):
    masked = jnp.where(allowed, scores, masked_score)
    new_max = jnp.maximum(running_max, jnp.max(masked, axis=-1))
    weights_now = jnp.where(allowed, jnp.exp(masked - new_max[:, :, None]), 0.0)
    shrink = jnp.exp(running_max - new_max)
    row_total = row_total * shrink + jnp.sum(weights_now, axis=-1)
    weighted = weighted * jnp.transpose(shrink)[:, :, None] + jnp.einsum(
        "hqk,khd->qhd",
        weights_now.astype(jnp.bfloat16),
        value_rows,
        preferred_element_type=jnp.float32,
    )
    return (new_max, row_total, weighted)


def score_grads(
    first_map, second_map, allowed, lse_pair, delta_pair, grad_rows, value_rows, lambda_value
):
    first_prob = jnp.where(
        allowed, jnp.exp(first_map - jnp.transpose(lse_pair[0])[:, :, None]), 0.0
    )
    second_prob = jnp.where(
        allowed, jnp.exp(second_map - jnp.transpose(lse_pair[1])[:, :, None]), 0.0
    )
    value_dot = jnp.einsum(
        "qhd,khd->hqk", grad_rows, value_rows, preferred_element_type=jnp.float32
    )
    first_grad = (first_prob * (value_dot - jnp.transpose(delta_pair[0])[:, :, None])).astype(
        jnp.bfloat16
    )
    second_grad = (
        second_prob * (-lambda_value * value_dot - jnp.transpose(delta_pair[1])[:, :, None])
    ).astype(jnp.bfloat16)
    return (first_prob, second_prob, first_grad, second_grad)


def tp_reduce(partial_rows, row_count):
    summed = lax.psum(partial_rows.astype(jnp.bfloat16), "tp").astype(jnp.float32)
    return lax.dynamic_slice_in_dim(summed, lax.axis_index("tp") * row_count, row_count, 0)


def key_fold(key_value, own_pos, combine, initial):
    return combine(
        initial,
        (
            lax.all_gather(key_value, ("seq", "tp"), axis=0, tiled=True),
            lax.all_gather(own_pos, ("seq", "tp"), axis=0, tiled=True),
        ),
        jnp.int32(0),
    )


def query_fold(query_pack, stats, own_pos, combine, initial):
    return combine(
        initial,
        (
            lax.all_gather(query_pack, ("seq", "tp"), axis=0, tiled=True),
            lax.all_gather(stats.astype(jnp.bfloat16), ("seq", "tp"), axis=0, tiled=True).astype(
                jnp.float32
            ),
            lax.all_gather(own_pos, ("seq", "tp"), axis=0, tiled=True),
        ),
        jnp.int32(0),
    )


def split_heads(packed):
    piece_rows = packed.shape[0]
    return (packed[:, :HW].reshape(piece_rows, H, VW), packed[:, HW:].reshape(piece_rows, H, VW))


def body(
    inputs,
    positions,
    attn_gain,
    w_query,
    w_key,
    w_value,
    w_out,
    lambda_params,
    sub_gain,
    ffn_gain,
    w_gate,
    w_up,
    w_down,
    cotangent,
):
    row_count = inputs.shape[0]
    score_scale = HALF ** (-0.5)
    inputs_f = inputs.astype(jnp.float32)
    attn_scale = rms_scale(inputs_f)
    attn_normed = (inputs_f * attn_scale * attn_gain).astype(jnp.bfloat16)
    queries = jnp.dot(attn_normed, w_query, preferred_element_type=jnp.float32).astype(jnp.bfloat16)
    key_rows = jnp.dot(attn_normed, w_key, preferred_element_type=jnp.float32).astype(jnp.bfloat16)
    value_rows = jnp.dot(attn_normed, w_value, preferred_element_type=jnp.float32).astype(
        jnp.bfloat16
    )
    query_heads = queries.reshape(row_count, H, VW)
    key_heads = key_rows.reshape(row_count, H, VW)
    value_heads = value_rows.reshape(row_count, H, VW)
    first_exp = jnp.exp(jnp.sum(lambda_params[0] * lambda_params[1]))
    second_exp = jnp.exp(jnp.sum(lambda_params[2] * lambda_params[3]))
    lambda_value = first_exp - second_exp + lambda_init
    key_value = jnp.concatenate([key_rows, value_rows], axis=1)

    def attend_piece(state_now, shard_part, start_row):
        part_keys, part_values = split_heads(shard_part[0])
        part_pos = shard_part[1]
        block_rows = math.gcd(part_keys.shape[0], 1024)

        def attend_advance(state_in, block_index):
            lower_row = block_index * block_rows
            block_keys = lax.dynamic_slice_in_dim(part_keys, lower_row, block_rows, 0)
            block_values = lax.dynamic_slice_in_dim(part_values, lower_row, block_rows, 0)
            block_pos = lax.dynamic_slice_in_dim(part_pos, lower_row, block_rows, 0)
            allowed = (block_pos[None, :] <= positions[:, None])[None]
            first_map, second_map = block_scores(query_heads, block_keys)
            first_state = online(
                state_in[0], state_in[2], state_in[4], first_map, allowed, block_values
            )
            second_state = online(
                state_in[1], state_in[3], state_in[5], second_map, allowed, block_values
            )
            return (
                (
                    first_state[0],
                    second_state[0],
                    first_state[1],
                    second_state[1],
                    first_state[2],
                    second_state[2],
                ),
                None,
            )

        state_out, unused = lax.scan(
            attend_advance, state_now, jnp.arange(part_keys.shape[0] // block_rows)
        )
        return state_out

    start_max = jnp.full((H, row_count), masked_score, jnp.float32)
    start_total = jnp.zeros((H, row_count), jnp.float32)
    start_sum = jnp.zeros((row_count, H, VW), jnp.float32)
    start_state = (start_max, start_max, start_total, start_total, start_sum, start_sum)
    folded = key_fold(key_value, positions, attend_piece, start_state)
    first_mix = folded[4] / jnp.transpose(folded[2])[:, :, None]
    second_mix = folded[5] / jnp.transpose(folded[3])[:, :, None]
    first_lse = jnp.transpose(folded[0] + jnp.log(folded[2]))
    second_lse = jnp.transpose(folded[1] + jnp.log(folded[3]))
    heads_out = first_mix - lambda_value * second_mix
    head_scale = rms_scale(heads_out)
    head_gain = sub_gain * (1.0 - lambda_init)
    mixed_heads = (heads_out * head_scale * head_gain).reshape(row_count, HW).astype(jnp.bfloat16)
    middle = inputs_f + jnp.dot(mixed_heads, w_out, preferred_element_type=jnp.float32)
    ffn_scale = rms_scale(middle)
    ffn_in = (middle * ffn_scale * ffn_gain).astype(jnp.bfloat16)
    ffn_rows, cotangent_rows = (
        lax.all_gather(ffn_in, "tp", axis=0, tiled=True),
        lax.all_gather(cotangent, "tp", axis=0, tiled=True),
    )
    gate_proj = jnp.dot(ffn_rows, w_gate, preferred_element_type=jnp.float32)
    up_proj = jnp.dot(ffn_rows, w_up, preferred_element_type=jnp.float32)
    gate_sig = jax.nn.sigmoid(gate_proj)
    gate_act = gate_proj * gate_sig
    hidden = (gate_act * up_proj).astype(jnp.bfloat16)
    ffn_out = tp_reduce(jnp.dot(hidden, w_down, preferred_element_type=jnp.float32), row_count)
    output = (middle + ffn_out).astype(jnp.bfloat16)
    down_part = jnp.einsum("rf,rd->fd", hidden, cotangent_rows, preferred_element_type=jnp.float32)
    hidden_grad = jnp.einsum(
        "rd,fd->rf", cotangent_rows, w_down, preferred_element_type=jnp.float32
    )
    gate_rows_grad = (
        hidden_grad * up_proj * gate_sig * (1.0 + gate_proj * (1.0 - gate_sig))
    ).astype(jnp.bfloat16)
    up_rows_grad = (hidden_grad * gate_act).astype(jnp.bfloat16)
    gate_part = jnp.einsum(
        "rd,rf->df", ffn_rows, gate_rows_grad, preferred_element_type=jnp.float32
    )
    up_part = jnp.einsum("rd,rf->df", ffn_rows, up_rows_grad, preferred_element_type=jnp.float32)
    ffn_partial = jnp.einsum(
        "rf,df->rd", gate_rows_grad, w_gate, preferred_element_type=jnp.float32
    ) + jnp.einsum("rf,df->rd", up_rows_grad, w_up, preferred_element_type=jnp.float32)
    ffn_in_grad = tp_reduce(ffn_partial, row_count)
    ffn_gain_part = jnp.sum(ffn_in_grad * middle * ffn_scale, axis=0)
    middle_grad = cotangent.astype(jnp.float32) + rms_back(middle, ffn_scale, ffn_gain, ffn_in_grad)
    branch_grad = middle_grad.astype(jnp.bfloat16)
    out_part = jnp.einsum("rc,rd->cd", mixed_heads, branch_grad, preferred_element_type=jnp.float32)
    mixed_grad = jnp.einsum(
        "rd,cd->rc", branch_grad, w_out, preferred_element_type=jnp.float32
    ).reshape(row_count, H, VW)
    sub_gain_part = jnp.sum(mixed_grad * heads_out * head_scale * (1.0 - lambda_init), axis=(0, 1))
    heads_grad = rms_back(heads_out, head_scale, head_gain, mixed_grad).astype(jnp.bfloat16)
    heads_grad_f = heads_grad.astype(jnp.float32)
    lambda_part = -jnp.sum(heads_grad_f * second_mix)
    first_delta = jnp.sum(heads_grad_f * first_mix, axis=-1)
    second_delta = -lambda_value * jnp.sum(heads_grad_f * second_mix, axis=-1)
    own_lse = (first_lse, second_lse)
    own_delta = (first_delta, second_delta)

    def query_grad_piece(state_now, shard_part, start_row):
        part_keys, part_values = split_heads(shard_part[0])
        part_pos = shard_part[1]
        block_rows = math.gcd(part_keys.shape[0], 1024)

        def query_advance(state_in, block_index):
            lower_row = block_index * block_rows
            block_keys = lax.dynamic_slice_in_dim(part_keys, lower_row, block_rows, 0)
            block_values = lax.dynamic_slice_in_dim(part_values, lower_row, block_rows, 0)
            block_pos = lax.dynamic_slice_in_dim(part_pos, lower_row, block_rows, 0)
            allowed = (block_pos[None, :] <= positions[:, None])[None]
            first_map, second_map = block_scores(query_heads, block_keys)
            grads_now = score_grads(
                first_map,
                second_map,
                allowed,
                own_lse,
                own_delta,
                heads_grad,
                block_values,
                lambda_value,
            )
            new_first = (
                state_in[0]
                + jnp.einsum(
                    "hqk,khd->qhd",
                    grads_now[2],
                    block_keys[:, :, :HALF],
                    preferred_element_type=jnp.float32,
                )
                * score_scale
            )
            new_second = (
                state_in[1]
                + jnp.einsum(
                    "hqk,khd->qhd",
                    grads_now[3],
                    block_keys[:, :, HALF:],
                    preferred_element_type=jnp.float32,
                )
                * score_scale
            )
            return ((new_first, new_second), None)

        state_out, unused = lax.scan(
            query_advance, state_now, jnp.arange(part_keys.shape[0] // block_rows)
        )
        return state_out

    zero_half = jnp.zeros((row_count, H, HALF), jnp.float32)
    query_state = key_fold(key_value, positions, query_grad_piece, (zero_half, zero_half))
    query_pack = jnp.concatenate([queries, heads_grad.reshape(row_count, HW)], axis=1)
    stats = jnp.concatenate([first_lse, second_lse, first_delta, second_delta], axis=1)

    def key_grad_piece(state_now, shard_part, start_row):
        part_queries, part_grads = split_heads(shard_part[0])
        part_stats = shard_part[1]
        part_pos = shard_part[2]
        block_rows = math.gcd(part_queries.shape[0], 1024)

        def key_advance(state_in, block_index):
            lower_row = block_index * block_rows
            block_queries = lax.dynamic_slice_in_dim(part_queries, lower_row, block_rows, 0)
            block_grads = lax.dynamic_slice_in_dim(part_grads, lower_row, block_rows, 0)
            block_stats = lax.dynamic_slice_in_dim(part_stats, lower_row, block_rows, 0)
            block_pos = lax.dynamic_slice_in_dim(part_pos, lower_row, block_rows, 0)
            allowed = (positions[None, :] <= block_pos[:, None])[None]
            first_map, second_map = block_scores(block_queries, key_heads)
            lse_pair = (block_stats[:, :H], block_stats[:, H : 2 * H])
            delta_pair = (block_stats[:, 2 * H : 3 * H], block_stats[:, 3 * H :])
            grads_now = score_grads(
                first_map,
                second_map,
                allowed,
                lse_pair,
                delta_pair,
                block_grads,
                value_heads,
                lambda_value,
            )
            new_first = (
                state_in[0]
                + jnp.einsum(
                    "hbk,bhd->khd",
                    grads_now[2],
                    block_queries[:, :, :HALF],
                    preferred_element_type=jnp.float32,
                )
                * score_scale
            )
            new_second = (
                state_in[1]
                + jnp.einsum(
                    "hbk,bhd->khd",
                    grads_now[3],
                    block_queries[:, :, HALF:],
                    preferred_element_type=jnp.float32,
                )
                * score_scale
            )
            new_value = (
                state_in[2]
                + jnp.einsum(
                    "hbk,bhd->khd",
                    grads_now[0].astype(jnp.bfloat16),
                    block_grads,
                    preferred_element_type=jnp.float32,
                )
                - lambda_value
                * jnp.einsum(
                    "hbk,bhd->khd",
                    grads_now[1].astype(jnp.bfloat16),
                    block_grads,
                    preferred_element_type=jnp.float32,
                )
            )
            return ((new_first, new_second, new_value), None)

        state_out, unused = lax.scan(
            key_advance, state_now, jnp.arange(part_queries.shape[0] // block_rows)
        )
        return state_out

    zero_full = jnp.zeros((row_count, H, VW), jnp.float32)
    key_state = query_fold(
        query_pack, stats, positions, key_grad_piece, (zero_half, zero_half, zero_full)
    )
    query_rows_grad = (
        jnp.concatenate([query_state[0], query_state[1]], axis=2)
        .reshape(row_count, HW)
        .astype(jnp.bfloat16)
    )
    key_rows_grad = (
        jnp.concatenate([key_state[0], key_state[1]], axis=2)
        .reshape(row_count, HW)
        .astype(jnp.bfloat16)
    )
    value_rows_grad = key_state[2].reshape(row_count, HW).astype(jnp.bfloat16)
    query_part = jnp.einsum(
        "rd,rc->dc", attn_normed, query_rows_grad, preferred_element_type=jnp.float32
    )
    key_part = jnp.einsum(
        "rd,rc->dc", attn_normed, key_rows_grad, preferred_element_type=jnp.float32
    )
    value_part = jnp.einsum(
        "rd,rc->dc", attn_normed, value_rows_grad, preferred_element_type=jnp.float32
    )
    normed_grad = (
        jnp.einsum("rc,dc->rd", query_rows_grad, w_query, preferred_element_type=jnp.float32)
        + jnp.einsum("rc,dc->rd", key_rows_grad, w_key, preferred_element_type=jnp.float32)
        + jnp.einsum("rc,dc->rd", value_rows_grad, w_value, preferred_element_type=jnp.float32)
    )
    attn_gain_part = jnp.sum(normed_grad * inputs_f * attn_scale, axis=0)
    input_grad = middle_grad + rms_back(inputs_f, attn_scale, attn_gain, normed_grad)
    lambda_total, sub_gain_grad = lax.psum((lambda_part, sub_gain_part), ("seq", "tp"))
    attn_grads = (
        lax.psum_scatter(attn_gain_part, ("seq", "tp"), scatter_dimension=0, tiled=True),
        lax.psum_scatter(query_part, ("seq", "tp"), scatter_dimension=0, tiled=True),
        lax.psum_scatter(key_part, ("seq", "tp"), scatter_dimension=0, tiled=True),
        lax.psum_scatter(value_part, ("seq", "tp"), scatter_dimension=0, tiled=True),
        lax.psum_scatter(out_part, ("seq", "tp"), scatter_dimension=0, tiled=True),
        lax.psum_scatter(ffn_gain_part, ("seq", "tp"), scatter_dimension=0, tiled=True),
    )
    ffn_grads = (
        lax.psum_scatter(
            gate_part.astype(jnp.bfloat16), "seq", scatter_dimension=0, tiled=True
        ).astype(jnp.float32),
        lax.psum_scatter(
            up_part.astype(jnp.bfloat16), "seq", scatter_dimension=0, tiled=True
        ).astype(jnp.float32),
        lax.psum_scatter(
            down_part.astype(jnp.bfloat16), "seq", scatter_dimension=1, tiled=True
        ).astype(jnp.float32),
    )
    lambda_grads = jnp.stack(
        [
            lambda_total * first_exp * lambda_params[1],
            lambda_total * first_exp * lambda_params[0],
            -lambda_total * second_exp * lambda_params[3],
            -lambda_total * second_exp * lambda_params[2],
        ]
    )
    lambda_norm = jnp.sqrt(jnp.sum(lambda_grads * lambda_grads))
    return (
        output,
        input_grad,
        attn_grads[0],
        attn_grads[1],
        attn_grads[2],
        attn_grads[3],
        attn_grads[4],
        lambda_grads,
        sub_gain_grad,
        attn_grads[5],
        ffn_grads[0],
        ffn_grads[1],
        ffn_grads[2],
        lambda_total,
        lambda_norm,
    )


def solution(mesh):
    placed = (
        P(("seq", "tp"), None),
        P(("seq", "tp")),
        P(),
        P(),
        P(),
        P(),
        P(),
        P(),
        P(),
        P(),
        P(None, "tp"),
        P(None, "tp"),
        P("tp", None),
        P(("seq", "tp"), None),
    )
    return jax.shard_map(
        body,
        mesh=mesh,
        in_specs=placed,
        out_specs=(
            P(("seq", "tp"), None),
            P(("seq", "tp"), None),
            P(("seq", "tp")),
            P(("seq", "tp"), None),
            P(("seq", "tp"), None),
            P(("seq", "tp"), None),
            P(("seq", "tp"), None),
            P(),
            P(),
            P(("seq", "tp")),
            P("seq", "tp"),
            P("seq", "tp"),
            P("tp", "seq"),
            P(),
            P(),
        ),
        check_vma=False,
    )
```

profile of v0, /device:TPU:0, one launch (start us, length us, event | category | flops | bytes accessed | tf_op | source)
XLA Modules:
  0.0 1411.6 jit_solution(14607754359591767426)
XLA Ops:
  25.2 72.7 %all-gather = s32[32,1,128]{2,1,0:T(1,128)} all-gather(s32[1,1,128]{2,1,0:T(1,128)} %bitcast.258), channel_id=1, replica_groups=mesh['seq'=8,'tp'=4] {'seq','tp'}, dimensions={0}, use_global_device_ids=true | all-gather | bytes 16896 | tf_op jit(solution)/shard_map/all_gather | solution.py:98
  99.1 75.0 %all-gather.6.cloned.1.call-done = bf16[4096,3072]{1,0:T(8,128)(2,1)} async-done(((bf16[128,3072]{1,0:T(8,128)(2,1)}), bf16[4096,3072]{1,0:T(8,128)(2,1)}) %all-gather.6.cloned.1.call-update) | async-done | bytes 25165840 | tf_op jit(solution)/shard_map/all_gather | solution.py:97
  174.1 17.1 %fusion.259 = (bf16[4096,1536]{1,0:T(8,128)(2,1)}, bf16[4096,1536]{1,0:T(8,128)(2,1)}) fusion(bf16[4096,3072]{1,0:T(8,128)(2,1)} %all-gather.6.cloned.1.call-done), kind=kLoop, calls=%fused_computation.245 | loop fusion | bytes 50331648 | tf_op jit(solution)/shard_map/slice | solution.py:120
  191.2 16.7 %copy.75 = bf16[4096,1536]{0,1:T(8,128)(2,1)} copy(bf16[4096,1536]{1,0:T(8,128)(2,1)} %get-tuple-element.761) | data formatting | bytes 25165824 | tf_op jit(solution)/shard_map/slice | solution.py:120
  207.9 15.7 %copy.77 = bf16[4096,1536]{0,1:T(8,128)(2,1)} copy(bf16[4096,1536]{1,0:T(8,128)(2,1)} %get-tuple-element.760) | data formatting | bytes 25165824 | tf_op jit(solution)/shard_map/slice | solution.py:120
  224.2 145.1 %while.52 = (s32[]{:T(128)}, f32[12,128]{1,0:T(8,128)S(1)}, f32[12,128]{1,0:T(8,128)S(1)}, f32[12,128]{1,0:T(8,128)}, f32[12,128]{1,0:T(8,128)}, /*index=5*/f32[...) while((s32[]{:T(128)}, f32[12,128]{1,0:T(8,128)S(1)}, ...), condition=%wide.region_6.7_spmd.clone, body=%wide.region_1.6_spmd.clone.sunk | while | flops 1250183168 | bytes 115127392 | solution.py:187
  228.3 5.2 fusion.352
  233.5 8.7 fusion.353
  243.6 6.3 fusion.356
  264.6 5.2 fusion.352
  269.7 8.7 fusion.353
  279.9 6.3 fusion.356
  300.8 5.2 fusion.352
  306.0 8.7 fusion.353
  316.1 6.3 fusion.356
  337.1 5.2 fusion.352
  342.3 8.7 fusion.353
  352.4 6.3 fusion.356
  379.6 28.1 %all-gather.8.cloned.1.call-done = bf16[512,1536]{1,0:T(8,128)(2,1)} async-done(((bf16[128,1536]{1,0:T(8,128)(2,1)}), bf16[512,1536]{1,0:T(8,128)(2,1)}) %all-gather.8.cloned.1.call-update) | async-done | bytes 1572880 | tf_op jit(solution)/shard_map/all_gather | solution.py:209
  407.7 5.6 fusion.260
  416.5 24.0 %all-gather.10.cloned.1.call-done = bf16[512,1536]{1,0:T(8,128)(2,1)} async-done(((bf16[128,1536]{1,0:T(8,128)(2,1)}), bf16[512,1536]{1,0:T(8,128)(2,1)}) %all-gather.10.cloned.1.call-update) | async-done | bytes 1572880 | tf_op jit(solution)/shard_map/all_gather | solution.py:210
  440.5 5.2 multiply_convert_fusion.16
  454.3 87.5 %all-reduce.6.cloned.1.call-done = (bf16[512,1536]{1,0:T(8,128)(2,1)}, bf16[512,1536]{1,0:T(8,128)(2,1)}) async-done(((bf16[512,1536]{1,0:T(8,128)(2,1)}, bf16[512,1536]{1,0:T(8,128)(2,1)}), (bf16[512,1536]{1,0:T(8,128)(2,1)}, bf16[512,1536]{1,0:T(8,128)(2,1)})) %all-reduce.6.cloned.1.call-update) | async-done | bytes 3145744 | tf_op jit(solution)/shard_map/psum | solution.py:89
  554.7 5.4 convolution_convert_fusion.2
  565.6 5.3 convolution_convert_fusion
  571.3 83.9 %while.53 = (s32[]{:T(128)}, f32[128,12,64]{0,2,1:T(8,128)S(1)}, f32[128,12,64]{0,2,1:T(8,128)S(1)}, s32[4]{0:T(128)S(1)}, bf16[4096,12,128]{0,2,1:T(8,128)(2,1)...) while((s32[]{:T(128)}, f32[128,12,64]{0,2,1:T(8,128)S(1)}, ...), condition=%wide.region_18.19_spmd.clone, body=%wide.region_17.18_spmd.clone.sunk | while | flops 1229127680 | bytes 31114516 | solution.py:295
  572.6 5.6 fusion.370
  579.1 6.4 fusion.371
  585.5 6.7 fusion.372
  593.5 5.6 fusion.370
  600.0 6.4 fusion.371
  606.4 6.6 fusion.372
  614.3 5.8 fusion.370
  621.0 6.5 fusion.371
  627.5 6.8 fusion.372
  635.5 5.6 fusion.370
  642.0 6.5 fusion.371
  648.5 6.7 fusion.372
  663.0 73.5 %all_gather.26 = bf16[4096,48]{0,1:T(8,128)(2,1)S(1)} all-gather(bf16[128,48]{0,1:T(8,128)(2,1)S(1)} %pad_maximum_fusion.4), channel_id=1, replica_groups=mesh['seq'=8,'tp'=4] {'seq','tp'}, dimensions={0}, use_global_device_ids=true | all-gather | bytes 405504 | tf_op jit(solution)/shard_map/all_gather | solution.py:109
  741.8 17.2 %fusion.258 = (bf16[4096,1536]{1,0:T(8,128)(2,1)}, bf16[4096,1536]{1,0:T(8,128)(2,1)}) fusion(bf16[4096,3072]{1,0:T(8,128)(2,1)} %all-gather.12.cloned.1.call-done), kind=kLoop, calls=%fused_computation.244 | loop fusion | bytes 50331648 | tf_op jit(solution)/shard_map/slice | solution.py:120
  759.0 16.3 %copy.82 = bf16[4096,1536]{0,1:T(8,128)(2,1)} copy(bf16[4096,1536]{1,0:T(8,128)(2,1)} %get-tuple-element.759) | data formatting | bytes 25165824 | tf_op jit(solution)/shard_map/slice | solution.py:120
  775.3 16.9 %copy.84 = bf16[4096,1536]{0,1:T(8,128)(2,1)} copy(bf16[4096,1536]{1,0:T(8,128)(2,1)} %get-tuple-element.758) | data formatting | bytes 25165824 | tf_op jit(solution)/shard_map/slice | solution.py:120
  792.6 161.3 %while.54 = (s32[]{:T(128)}, f32[128,12,64]{0,2,1:T(8,128)S(1)}, f32[128,12,64]{0,2,1:T(8,128)}, f32[128,12,128]{0,2,1:T(8,128)S(1)}, s32[4]{0:T(128)}, /*index=...) while((s32[]{:T(128)}, f32[128,12,64]{0,2,1:T(8,128)S(1)}, ...), condition=%wide.region_20.21_spmd.clone, body=%wide.region_19.20_spmd.clone.sunk | while | flops 2047803392 | bytes 101234664 | solution.py:369
  794.6 5.7 fusion.385
  800.4 5.2 fusion.386
  806.6 7.6 fusion.387
  816.9 6.7 fusion.389
  834.6 5.8 fusion.385
  840.4 5.2 fusion.386
  846.6 7.9 fusion.387
  857.2 6.8 fusion.389
  875.2 5.9 fusion.385
  881.1 5.3 fusion.386
  887.4 7.5 fusion.387
  898.1 6.6 fusion.389
  915.8 5.8 fusion.385
  921.6 5.2 fusion.386
  927.8 7.7 fusion.387
  938.2 6.6 fusion.389
  982.8 5.7 fusion.241
  988.5 37.4 %all-reduce.2 = (f32[1536]{0:T(1024)}, f32[]{:T(128)}, f32[128]{0:T(128)}, f32[1536]{0:T(1024)}) all-reduce(f32[1536]{0:T(1024)} %get-tuple-element.641, f32[]{:T(128)S(6)} %neg.21, f32[128]{0:T(128)} %get-tuple-element.637, f32[1536]{0:T(1024)} %get-tuple-element.635), channel_id=2, replica_groups=mesh['seq'=8,'tp'=4] {'seq','tp'}, use_global_device_ids=true, to_apply=%region_23.24.clone | all-reduce | flops 3201 | bytes 25608
  1034.9 85.5 %reduce-scatter.14.cloned.1.call-done = f32[48,1536]{1,0:T(8,128)} async-done(((f32[1536,1536]{1,0:T(8,128)}), f32[48,1536]{1,0:T(8,128)}) %reduce-scatter.14.cloned.1.call-update) | async-done | bytes 294928 | tf_op jit(solution)/shard_map/reduce_scatter | solution.py:411
  1120.4 142.0 %reduce-scatter.10.cloned.1.call-done = f32[48,1536]{1,0:T(8,128)} async-done(((f32[1536,1536]{1,0:T(8,128)}), f32[48,1536]{1,0:T(8,128)}) %reduce-scatter.10.cloned.1.call-update) | async-done | bytes 294928 | tf_op jit(solution)/shard_map/reduce_scatter | solution.py:409
  1262.4 141.0 %reduce-scatter.12.cloned.1.call-done = f32[48,1536]{1,0:T(8,128)} async-done(((f32[1536,1536]{1,0:T(8,128)}), f32[48,1536]{1,0:T(8,128)}) %reduce-scatter.12.cloned.1.call-update) | async-done | bytes 294928 | tf_op jit(solution)/shard_map/reduce_scatter | solution.py:410
  (429 shorter events, 230.6 us)
Async XLA Ops:
  7.2 433.4 %copy-start = (bf16[1024,1536]{1,0:T(8,128)(2,1)S(1)}, bf16[1024,1536]{1,0:T(8,128)(2,1)}, u32[]{:S(2)}) copy-start(bf16[1024,1536]{1,0:T(8,128)(2,1)} %param.32) | copy-start | bytes 9437188
  7.2 166.9 %all-gather.6.cloned.1.call-start = ((), (), s32[]{:S(2)}) async-start(), calls=%async_computation.7 | async-start | bytes 25952256 | tf_op jit(solution)/shard_map/all_gather | solution.py:97
  9.2 7.3 copy-start.3
  16.4 391.3 %all-gather.8.cloned.1.call-start = ((), (), s32[]{:S(2)}) async-start(), calls=%async_computation.8 | async-start | bytes 1966080 | tf_op jit(solution)/shard_map/all_gather | solution.py:209
  243.5 6.4 copy-start.32
  243.5 6.4 copy-start.35
  243.5 6.5 copy-start.2
  243.6 6.5 copy-start.5
  243.6 6.7 copy-start.24
  243.6 11.4 slice-start
  279.8 6.4 copy-start.32
  279.8 6.4 copy-start.35
  279.8 6.5 copy-start.2
  279.8 6.5 copy-start.5
  279.8 6.7 copy-start.24
  279.9 11.4 slice-start
  316.1 6.4 copy-start.35
  316.1 6.5 copy-start.2
  316.1 6.5 copy-start.5
  316.1 6.7 copy-start.24
  316.1 11.4 slice-start
  352.4 6.4 copy-start.35
  352.4 6.5 copy-start.2
  352.4 6.5 copy-start.5
  352.4 6.7 copy-start.24
  352.4 11.4 slice-start
  369.3 8.2 copy-start.44
  378.4 62.2 %all-gather.10.cloned.1.call-start = ((), (), s32[]{:S(2)}) async-start(), calls=%async_computation.9 | async-start | bytes 1966080 | tf_op jit(solution)/shard_map/all_gather | solution.py:210
  379.1 162.7 %all-reduce.6.cloned.1.call-start = ((), (), s32[]{:S(2)}) async-start(), calls=%async_computation.18 | async-start | bytes 6291456 | tf_op jit(solution)/shard_map/psum | solution.py:89
  451.2 90.6 %copy-start.9 = (f32[128,1536]{1,0:T(8,128)S(1)}, f32[128,1536]{1,0:T(8,128)}, u32[]{:S(2)}) copy-start(f32[128,1536]{1,0:T(8,128)} %copy-done.8) | copy-start | bytes 2359300
  451.2 90.6 %copy-start.45 = (f32[1536]{0:T(1024)S(1)}, f32[1536]{0:T(1024)}, u32[]{:S(2)}) copy-start(f32[1536]{0:T(1024)} %param.29) | copy-start | bytes 18436
  451.2 90.6 %copy-start.57 = (f32[128]{0:T(128)S(1)}, f32[128]{0:T(128)}, u32[]{:S(2)}) copy-start(f32[128]{0:T(128)} %copy-done.56) | copy-start | bytes 1540
  451.2 92.5 %copy-start.28 = (bf16[128,1536]{1,0:T(8,128)(2,1)S(1)}, bf16[128,1536]{1,0:T(8,128)(2,1)}, u32[]{:S(2)}) copy-start(bf16[128,1536]{1,0:T(8,128)(2,1)} %param.33) | copy-start | bytes 1179652
  451.2 92.4 %copy-start.58 = (f32[128]{0:T(128)S(1)}, f32[128]{0:T(128)}, u32[]{:S(2)}) copy-start(f32[128]{0:T(128)} %get-tuple-element.775) | copy-start | bytes 1540
  454.3 95.7 %copy-start.11 = (f32[128,12,128]{0,2,1:T(8,128)S(1)}, f32[128,12,128]{0,2,1:T(8,128)}, u32[]{:S(2)}) copy-start(f32[128,12,128]{0,2,1:T(8,128)} %copy-done.10) | copy-start | bytes 2359300
  454.3 95.7 %copy-start.43 = (f32[128,12]{0,1:T(8,128)S(1)}, f32[128,12]{0,1:T(8,128)}, u32[]{:S(2)}) copy-start(f32[128,12]{0,1:T(8,128)} %copy-done.42) | copy-start | bytes 18436
  454.3 95.7 %copy-start.55 = (f32[128]{0:T(128)S(1)}, f32[128]{0:T(128)}, u32[]{:S(2)}) copy-start(f32[128]{0:T(128)} %broadcast_multiply_fusion.2) | copy-start | bytes 1540
  454.3 287.5 %all-gather.12.cloned.1.call-start = ((), (), s32[]{:S(2)}) async-start(), calls=%async_computation.10 | async-start | bytes 25952256 | tf_op jit(solution)/shard_map/all_gather | solution.py:108
  545.9 190.7 %copy-start.12 = (f32[128,1536]{1,0:T(8,128)}, f32[128,1536]{1,0:T(8,128)S(1)}, u32[]{:S(2)}) copy-start(f32[128,1536]{1,0:T(8,128)S(1)} %get-tuple-element.765) | copy-start | bytes 2359300
  545.9 7.6 copy-start.19
  554.5 417.9 %reduce-scatter.16.cloned.1.call-start = ((), (), s32[]{:S(2)}) async-start(), calls=%async_computation.15 | async-start | bytes 3538944 | tf_op jit(solution)/shard_map/reduce_scatter | solution.py:415
  560.1 414.3 %reduce-scatter.18.cloned.1.call-start = ((), (), s32[]{:S(2)}) async-start(), calls=%async_computation.16 | async-start | bytes 3538944 | tf_op jit(solution)/shard_map/reduce_scatter | solution.py:418
  564.9 411.4 %reduce-scatter.20.cloned.1.call-start = ((), (), s32[]{:S(2)}) async-start(), calls=%async_computation.17 | async-start | bytes 3538944 | tf_op jit(solution)/shard_map/reduce_scatter | solution.py:421
  570.9 463.9 %reduce-scatter.8.cloned.1.call-start = ((), (), s32[]{:S(2)}) async-start(), calls=%async_computation.11 | async-start | bytes 9732096 | tf_op jit(solution)/shard_map/reduce_scatter | solution.py:408
  571.3 84.8 %copy-start.29 = (f32[1536]{0:T(1024)S(1)}, f32[1536]{0:T(1024)}, u32[]{:S(2)}) copy-start(f32[1536]{0:T(1024)} %param.22) | copy-start | bytes 18436
  571.3 84.8 %copy-start.47 = (f32[128]{0:T(128)S(1)}, f32[128]{0:T(128)}, u32[]{:S(2)}) copy-start(f32[128]{0:T(128)} %copy-done.46) | copy-start | bytes 1540
  661.3 75.3 %copy-start.14 = (bf16[128,12,128]{0,2,1:T(8,128)(2,1)S(1)}, bf16[128,12,128]{0,2,1:T(8,128)(2,1)}, u32[]{:S(2)}) copy-start(bf16[128,12,128]{0,2,1:T(8,128)(2,1)} %copy-done.13) | copy-start | bytes 1179652
  661.3 459.1 %reduce-scatter.14.cloned.1.call-start = ((), (), s32[]{:S(2)}) async-start(), calls=%async_computation.14 | async-start | bytes 9732096 | tf_op jit(solution)/shard_map/reduce_scatter | solution.py:411
  741.6 520.9 %reduce-scatter.10.cloned.1.call-start = ((), (), s32[]{:S(2)}) async-start(), calls=%async_computation.12 | async-start | bytes 9732096 | tf_op jit(solution)/shard_map/reduce_scatter | solution.py:409
  775.3 17.4 %copy-start.31 = (f32[128,12,128]{0,2,1:T(8,128)S(1)}, f32[128,12,128]{0,2,1:T(8,128)}, u32[]{:S(2)}) copy-start(f32[128,12,128]{0,2,1:T(8,128)} %custom-call.10) | copy-start | bytes 2359300
  792.6 162.4 %copy-start.4 = (bf16[128,1536]{1,0:T(8,128)(2,1)S(1)}, bf16[128,1536]{1,0:T(8,128)(2,1)}, u32[]{:S(2)}) copy-start(bf16[128,1536]{1,0:T(8,128)(2,1)} %param.20) | copy-start | bytes 1179652
  792.6 162.4 %copy-start.30 = (f32[1536]{0:T(1024)S(1)}, f32[1536]{0:T(1024)}, u32[]{:S(2)}) copy-start(f32[1536]{0:T(1024)} %param.22) | copy-start | bytes 18436
  792.6 162.4 %copy-start.48 = (f32[128]{0:T(128)S(1)}, f32[128]{0:T(128)}, u32[]{:S(2)}) copy-start(f32[128]{0:T(128)} %copy-done.46) | copy-start | bytes 1540
  814.2 9.4 slice-start.2
  816.9 6.7 slice-start.3
  854.5 9.6 slice-start.2
  857.2 6.9 slice-start.3
  894.9 9.8 slice-start.2
  898.1 6.7 slice-start.3
  935.5 9.3 slice-start.2
  938.2 6.7 slice-start.3
  960.2 443.2 %reduce-scatter.12.cloned.1.call-start = ((), (), s32[]{:S(2)}) async-start(), calls=%async_computation.13 | async-start | bytes 9732096 | tf_op jit(solution)/shard_map/reduce_scatter | solution.py:410
  978.3 51.5 %copy-start.54 = (f32[4,64]{1,0:T(4,128)S(1)}, f32[4,64]{1,0:T(4,128)}, u32[]{:S(2)}) copy-start(f32[4,64]{1,0:T(4,128)} %param.27) | copy-start | bytes 3076
  978.3 425.1 %copy-start.1 = (bf16[1024,1536]{1,0:T(8,128)(2,1)S(1)}, bf16[1024,1536]{1,0:T(8,128)(2,1)}, u32[]{:S(2)}) copy-start(bf16[1024,1536]{1,0:T(8,128)(2,1)} %param.32) | copy-start | bytes 9437188
  (67 other events, 250.2 us)
Sparse Core Ops, SparseCore 0:
  16.5 157.5 all-gather.5
  378.5 29.1 all-gather.7
  409.5 30.9 all-gather.9
  454.4 87.3 all-reduce.5
  554.6 157.4 all-gather.11
  714.3 38.7 reduce-scatter.15
  755.5 39.7 reduce-scatter.17
  797.7 39.4 reduce-scatter.19
  844.6 134.7 reduce-scatter.7
  985.8 134.5 reduce-scatter.13
  1127.9 134.5 reduce-scatter.9
  1268.8 134.5 reduce-scatter.11
where the time goes:
time: 1420 us; the launch traced here: 1410 us
  waiting for transfers between devices  584 us (41%)
  matrix products  406 us (29%)
  blocking collectives  184 us (13%)
  local copies, waits for them, and re-layouts  138 us (10%)
  other arithmetic  69.3 us (5%)
  between operations  20.5 us (1%)
    reduce_scatter x1, waiting for transfers between devices, body(): lax.psum_scatter(key_part, ('seq', 'tp'), scatter_dimension=0, tiled=True)  142 us
    reduce_scatter x1, waiting for transfers between devices, body(): lax.psum_scatter(value_part, ('seq', 'tp'), scatter_dimension=0, tiled=True)  141 us
    psum x1, waiting for transfers between devices, tp_reduce(): lax.psum(partial_rows.astype(jnp.bfloat16), 'tp').astype(jnp.float32)  87.5 us
    reduce_scatter x1, waiting for transfers between devices, body(): lax.psum_scatter(out_part, ('seq', 'tp'), scatter_dimension=0, tiled=True)  85.5 us
    all_gather x1, waiting for transfers between devices, key_fold(): lax.all_gather(key_value, ('seq', 'tp'), axis=0, tiled=True)  75 us
    all_gather x1, blocking collectives, query_fold(): lax.all_gather(stats.astype(jnp.bfloat16), ('seq', 'tp'), axis=0, tiled=T...  73.5 us
    all_gather x1, blocking collectives, key_fold(): lax.all_gather(own_pos, ('seq', 'tp'), axis=0, tiled=True)  72.7 us
    slice x4, local copies, waits for them, and re-layouts, split_heads(): packed[:, HW:].reshape(piece_rows, H, VW)  66.9 us
  transfers between devices with their start and end apart: 12, of which 7 were waited for; matrix products, arithmetic and copies ran while one was open for 26% of the time, Pallas kernels for 0%

commit v1 on v0

v1 whole, which is shorter than its diff:
```python
import functools
import math

import jax
import jax.numpy as jnp
from jax import lax
from jax.experimental import pallas as pl
from jax.experimental.pallas import tpu as pltpu
from jax.sharding import PartitionSpec as P

H = 12
HALF = 64
VW = 128
HW = 1536

eps = 1e-05
lambda_init = 0.8 - 0.6 * math.exp(-3.3)
masked_score = -1e30
MESH = pl.DeviceIdType.MESH
ANY = pl.BlockSpec(memory_space=pl.ANY)
VMEM = pl.BlockSpec(memory_space=pltpu.VMEM)
SMEM = pl.BlockSpec(memory_space=pltpu.SMEM)
bf16 = jnp.bfloat16
f32 = jnp.float32
vmem_cap = 60 * 1024 * 1024


def dot(left, right):
    return jnp.dot(left, right, preferred_element_type=f32)


def dot_tn(left, right):
    return lax.dot_general(left, right, (((0,), (0,)), ((), ())), preferred_element_type=f32)


def dot_nt(left, right):
    return lax.dot_general(left, right, (((1,), (1,)), ((), ())), preferred_element_type=f32)


def rms_scale(values):
    return lax.rsqrt(jnp.mean(values * values, axis=-1, keepdims=True) + eps)


def rms_back(values, inv_rms, gain_vec, upstream):
    weighted = upstream * gain_vec
    inner_mean = jnp.mean(weighted * values, axis=-1, keepdims=True)
    return inv_rms * weighted - values * (inv_rms * inv_rms * inv_rms) * inner_mean


class Place:
    def __init__(self, seq, tp):
        self.seq, self.tp, self.n = seq, tp, seq * tp
        self.per = -(-H // (seq // 2))
        assert self.per <= tp and seq % 2 == 0

    def me(self):
        s, t = lax.axis_index("seq"), lax.axis_index("tp")
        head = (s // 2) * self.per + t
        active = jnp.logical_and(t < self.per, head < H)
        return s, t, lax.rem(s, 2), head, active

    def head_device(self, index):
        head, core = index // 2, lax.rem(index, 2)
        return 2 * (head // self.per) + core, lax.rem(head, self.per)

    def device(self, linear):
        return linear // self.tp, lax.rem(linear, self.tp)


def remote(src, dst, send, recv, where):
    return pltpu.make_async_remote_copy(
        src_ref=src, dst_ref=dst, send_sem=send, recv_sem=recv, device_id=where, device_id_type=MESH
    )


def loop(count, step):
    def one(k, carry):
        step(k)
        return carry

    lax.fori_loop(0, count, one, 0)


class Dispatch:
    def __init__(self, place):
        self.p = place
        self.sems = [2 * H, place.n, 1]

    def start(self, x, o, send, recv, here):
        p = self.p
        s, t, c, head, active = p.me()
        lin = s * p.tp + t

        def step(k):
            index = lax.rem(k + lin, 2 * H)
            ds, dt = p.head_device(index)
            mine = jnp.logical_and(ds == s, dt == t)

            @pl.when(jnp.logical_not(mine))
            def _():
                remote(
                    x.at[index // 2, lax.rem(index, 2)],
                    o.at[lin],
                    send.at[index],
                    recv.at[lin],
                    (ds, dt),
                ).start()

            @pl.when(mine)
            def _():
                pltpu.make_async_copy(
                    x.at[index // 2, lax.rem(index, 2)], o.at[lin], here.at[0]
                ).start()

        loop(2 * H, step)

    def finish(self, x, o, send, recv, here, arrived=None):
        p = self.p
        s, t, c, head, active = p.me()
        lin = s * p.tp + t

        @pl.when(active)
        def _():
            pltpu.make_async_copy(x.at[0, 0], o.at[lin], here.at[0]).wait()
            if arrived is not None:
                arrived(lin)

            def got(k):
                other = lax.rem(lin + 1 + k, p.n)
                remote(o.at[other], o.at[other], send.at[0], recv.at[other], (s, t)).wait_recv()
                if arrived is not None:
                    arrived(other)

            loop(p.n - 1, got)

        def sent(k):
            ds, dt = p.head_device(k)

            @pl.when(jnp.logical_not(jnp.logical_and(ds == s, dt == t)))
            def _():
                remote(
                    x.at[k // 2, lax.rem(k, 2)], o.at[0], send.at[k], recv.at[0], (ds, dt)
                ).wait_send()

        loop(2 * H, sent)


class Collect:
    def __init__(self, place, halves=False, grouped=False):
        self.p = place
        self.halves = halves
        self.grouped = grouped
        self.sems = [place.n, 2 * H, 1]

    def start(self, x, o, send, recv, here):
        p = self.p
        s, t, c, head, active = p.me()
        lin = s * p.tp + t
        count = p.n // 2 if self.halves else p.n

        @pl.when(active)
        def _():
            def step(k):
                slot = lax.rem(k + lin, count)
                other = slot + c * count if self.halves else slot
                into = o.at[lax.rem(other, p.tp)] if self.grouped else o
                into = into.at[head] if self.halves else into.at[head, c]

                @pl.when(other != lin)
                def _():
                    remote(
                        x.at[slot], into, send.at[slot], recv.at[head * 2 + c], p.device(other)
                    ).start()

                @pl.when(other == lin)
                def _():
                    pltpu.make_async_copy(x.at[slot], into, here.at[0]).start()

            loop(count, step)

    def finish(self, x, o, send, recv, here):
        p = self.p
        s, t, c, head, active = p.me()
        lin = s * p.tp + t
        count = p.n // 2 if self.halves else p.n
        half = lin // count if self.halves else 0
        o = o.at[t] if self.grouped else o

        def got(k):
            index = 2 * k + half if self.halves else k
            into = o.at[k] if self.halves else o.at[k // 2, lax.rem(k, 2)]
            ds, dt = p.head_device(index)
            mine = jnp.logical_and(ds == s, dt == t)

            @pl.when(jnp.logical_not(mine))
            def _():
                remote(into, into, send.at[0], recv.at[index], (s, t)).wait_recv()

            @pl.when(mine)
            def _():
                pltpu.make_async_copy(x.at[0], into, here.at[0]).wait()

        loop(H if self.halves else 2 * H, got)

        @pl.when(active)
        def _():
            def sent(k):
                other = k + c * count if self.halves else k

                @pl.when(other != lin)
                def _():
                    remote(
                        x.at[k], x.at[k], send.at[k], recv.at[0], p.device(other)
                    ).wait_send()

            loop(count, sent)


class Everyone:
    def __init__(self, place, whole):
        self.p, self.whole = place, whole
        self.sems = [place.n, place.n, 1]

    def start(self, x, o, send, recv, here):
        p = self.p
        s, t = lax.axis_index("seq"), lax.axis_index("tp")
        lin = s * p.tp + t
        pltpu.make_async_copy(x if self.whole else x.at[lin], o.at[lin], here.at[0]).start()

        def step(k):
            other = lax.rem(lin + 1 + k, p.n)
            remote(
                x if self.whole else x.at[other],
                o.at[lin],
                send.at[other],
                recv.at[lin],
                p.device(other),
            ).start()

        loop(p.n - 1, step)

    def finish(self, x, o, send, recv, here):
        p = self.p
        s, t = lax.axis_index("seq"), lax.axis_index("tp")
        lin = s * p.tp + t
        pltpu.make_async_copy(x if self.whole else x.at[lin], o.at[lin], here.at[0]).wait()

        def done(k):
            other = lax.rem(lin + 1 + k, p.n)
            both = remote(
                x if self.whole else x.at[other],
                o.at[other],
                send.at[other],
                recv.at[other],
                p.device(other),
            )
            both.wait_recv()
            both.wait_send()

        loop(p.n - 1, done)


class Group:
    def __init__(self, place, whole):
        self.p, self.whole = place, whole
        self.sems = [place.tp, place.tp, 1]

    def start(self, x, o, send, recv, here):
        p = self.p
        s, t = lax.axis_index("seq"), lax.axis_index("tp")
        pltpu.make_async_copy(x if self.whole else x.at[t], o.at[t], here.at[0]).start()
        for k in range(1, p.tp):
            other = lax.rem(t + k, p.tp)
            remote(
                x if self.whole else x.at[other], o.at[t], send.at[other], recv.at[t], (s, other)
            ).start()

    def finish(self, x, o, send, recv, here):
        p = self.p
        s, t = lax.axis_index("seq"), lax.axis_index("tp")
        pltpu.make_async_copy(x if self.whole else x.at[t], o.at[t], here.at[0]).wait()
        for k in range(1, p.tp):
            other = lax.rem(t + k, p.tp)
            both = remote(
                x if self.whole else x.at[other],
                o.at[other],
                send.at[other],
                recv.at[other],
                (s, other),
            )
            both.wait_recv()
            both.wait_send()


def greet(place):
    s, t = lax.axis_index("seq"), lax.axis_index("tp")
    lin = s * place.tp + t
    barrier = pltpu.get_barrier_semaphore()

    def hello(k):
        pl.semaphore_signal(
            barrier,
            inc=1,
            device_id=place.device(lax.rem(lin + 1 + k, place.n)),
            device_id_type=MESH,
        )

    loop(place.n - 1, hello)
    pl.semaphore_wait(barrier, place.n - 1)


def moves(place, parts, arrays, shapes, ident, cost=0):
    count = len(parts)

    def kernel(*refs):
        ins, outs, sems = refs[:count], refs[count : 2 * count], refs[2 * count :]
        greet(place)
        for i, part in enumerate(parts):
            part.start(ins[i], outs[i], *sems[3 * i : 3 * i + 3])
        for i, part in enumerate(parts):
            part.finish(ins[i], outs[i], *sems[3 * i : 3 * i + 3])

    return pl.pallas_call(
        kernel,
        out_shape=[jax.ShapeDtypeStruct(s, a.dtype) for s, a in zip(shapes, arrays)],
        in_specs=[ANY] * count,
        out_specs=[ANY] * count,
        scratch_shapes=[pltpu.SemaphoreType.DMA((k,)) for part in parts for k in part.sems],
        compiler_params=pltpu.CompilerParams(collective_id=ident, has_side_effects=True),
    )(*arrays)


def send_heads(place, payload, run_pos, ident):
    n, rows = place.n, payload.shape[2]
    give, tell = Dispatch(place), Everyone(place, True)

    def kernel(x, r, own, sib, pos, *sems):
        s, t, c, head, active = place.me()
        send, recv = sems[6], sems[7]
        greet(place)
        give.start(x, own, *sems[:3])
        tell.start(r, pos, *sems[3:6])

        def pass_on(k):
            return remote(
                own.at[k, :, VW : 3 * VW], sib.at[k], send.at[k], recv.at[k], (s + 1 - 2 * c, t)
            )

        give.finish(x, own, *sems[:3], arrived=lambda k: pass_on(k).start())

        @pl.when(active)
        def _():
            def done(k):
                pass_on(k).wait_recv()
                pass_on(k).wait_send()

            loop(n, done)

        tell.finish(r, pos, *sems[3:6])

    return pl.pallas_call(
        kernel,
        out_shape=[
            jax.ShapeDtypeStruct((n, rows, 3 * VW), payload.dtype),
            jax.ShapeDtypeStruct((n, rows, 2 * VW), payload.dtype),
            jax.ShapeDtypeStruct((n,) + run_pos.shape, run_pos.dtype),
        ],
        in_specs=[ANY] * 2,
        out_specs=[ANY] * 3,
        scratch_shapes=[pltpu.SemaphoreType.DMA((k,)) for k in give.sems + tell.sems + [n, n]],
        compiler_params=pltpu.CompilerParams(collective_id=ident, has_side_effects=True),
    )(payload, run_pos)


def return_heads(place, mixed, ident):
    n = place.n
    back, share = Collect(place, grouped=True), Group(place, True)

    def kernel(x, o, *sems):
        t = lax.axis_index("tp")
        s = lax.axis_index("seq")
        greet(place)
        own = o.at[t]
        back.start(x, o, *sems[:3])
        back.finish(x, o, *sems[:3])
        send, recv = sems[3], sems[4]
        for k in range(1, place.tp):
            other = lax.rem(t + k, place.tp)
            remote(own, o.at[t], send.at[other], recv.at[t], (s, other)).start()
        for k in range(1, place.tp):
            other = lax.rem(t + k, place.tp)
            both = remote(own, o.at[other], send.at[other], recv.at[other], (s, other))
            both.wait_recv()
            both.wait_send()

    return pl.pallas_call(
        kernel,
        out_shape=jax.ShapeDtypeStruct((place.tp, H, 2) + mixed.shape[1:], mixed.dtype),
        in_specs=[ANY],
        out_specs=ANY,
        scratch_shapes=[pltpu.SemaphoreType.DMA((k,)) for k in back.sems + share.sems[:2]],
        compiler_params=pltpu.CompilerParams(collective_id=ident, has_side_effects=True),
    )(mixed)


def query_rows(n):
    return 256 if n <= 64 else 128


def two_maps(rows):
    lane = lax.broadcasted_iota(jnp.int32, rows.shape, 1)
    zero = jnp.zeros_like(rows)
    return jnp.concatenate(
        [jnp.where(lane < HALF, rows, zero), jnp.where(lane < HALF, zero, rows)], axis=0
    )


def fwd_kernel(n, order, core, lam, own, sib, gain, mixed, mix, lse, qs, ks, vs, score):
    qb = query_rows(n)
    kb_rows = 2 * qb
    c = core[0]
    lambda_value = lam[0]

    def sort(p):
        run = order[p]
        i, b = run // 2, lax.rem(run, 2)
        b = pl.multiple_of(32 * b, 32)
        mine = own[i, pl.ds(b, 32), :]
        other = sib[i, pl.ds(b, 32), :]
        qs[pl.ds(pl.multiple_of(32 * p, 32), 32), :] = mine[:, :VW] * jnp.asarray(0.125, bf16)
        low = pl.multiple_of(64 * p + 32 * c, 32)
        high = pl.multiple_of(64 * p + 32 * (1 - c), 32)
        ks[pl.ds(low, 32), :] = mine[:, VW : 2 * VW]
        vs[pl.ds(low, 32), :] = mine[:, 2 * VW :]
        ks[pl.ds(high, 32), :] = other[:, :VW]
        vs[pl.ds(high, 32), :] = other[:, VW:]

    loop(2 * n, sort)

    def block(j):
        at = pl.ds(pl.multiple_of(qb * j, qb), qb)
        q2 = two_maps(qs[at, :])

        def scores(kb):
            return dot_nt(q2, ks[pl.ds(pl.multiple_of(kb_rows * kb, kb_rows), kb_rows), :])

        def lanes(top, s):
            for i in range(kb_rows // 128):
                top = jnp.maximum(top, s[:, 128 * i : 128 * i + 128])
            return top

        def first(kb, top):
            s = scores(kb)
            score[:, pl.ds(pl.multiple_of(kb_rows * kb, kb_rows), kb_rows)] = s
            return lanes(top, s)

        top = lax.fori_loop(0, j, first, jnp.full((2 * qb, 128), masked_score, f32))
        s = scores(j)
        row = lax.broadcasted_iota(jnp.int32, s.shape, 0)
        row = lax.rem(row, qb)
        allowed = (
            lax.broadcasted_iota(jnp.int32, s.shape, 1)
            <= 64 * (row // 32) + lax.rem(row, 32) + 32 * c
        )
        s = jnp.where(allowed, s, masked_score)
        score[:, pl.ds(pl.multiple_of(kb_rows * j, kb_rows), kb_rows)] = s
        high = jnp.max(lanes(top, s), axis=1, keepdims=True)
        ones = jnp.ones((kb_rows, VW), bf16)

        def second(kb, acc):
            here = pl.ds(pl.multiple_of(kb_rows * kb, kb_rows), kb_rows)
            weights = jnp.exp(score[:, here] - high).astype(bf16)
            return acc + dot(weights, jnp.concatenate([vs[here, :], ones], axis=1))

        acc = lax.fori_loop(0, j + 1, second, jnp.zeros((2 * qb, 2 * VW), f32))
        total = acc[:, VW:]
        mixes = acc[:, :VW] / total
        lse[j] = jnp.transpose(high + jnp.log(total))[:8, :]
        mix[0, at, :] = mixes[:qb]
        mix[1, at, :] = mixes[qb:]
        out = mixes[:qb] - lambda_value * mixes[qb:]
        out = (out * rms_scale(out) * gain[...]).astype(bf16)
        for i in range(qb // 32):
            run = order[j * (qb // 32) + i]
            b = pl.multiple_of(32 * lax.rem(run, 2), 32)
            mixed[run // 2, pl.ds(b, 32), :] = out[32 * i : 32 * i + 32]

    loop(n * 64 // qb, block)


def attend(place, order, core, lam, own, sib, gain):
    n = place.n
    rows = 64 * n
    qb = query_rows(n)
    return pl.pallas_call(
        functools.partial(fwd_kernel, n),
        out_shape=[
            jax.ShapeDtypeStruct((n, 64, VW), bf16),
            jax.ShapeDtypeStruct((2, rows, VW), f32),
            jax.ShapeDtypeStruct((rows // qb, 8, 2 * qb), f32),
            jax.ShapeDtypeStruct((rows, VW), bf16),
            jax.ShapeDtypeStruct((2 * rows, VW), bf16),
            jax.ShapeDtypeStruct((2 * rows, VW), bf16),
        ],
        in_specs=[SMEM, SMEM, SMEM, VMEM, VMEM, VMEM],
        out_specs=[VMEM] * 6,
        scratch_shapes=[pltpu.VMEM((2 * qb, 2 * rows), f32)],
        compiler_params=pltpu.CompilerParams(vmem_limit_bytes=vmem_cap),
        cost_estimate=pl.CostEstimate(
            flops=12 * rows * rows * VW, bytes_accessed=12 * rows * VW, transcendentals=0
        ),
    )(order, core, lam, own, sib, gain)


def bwd_kernel(
    n,
    order,
    core,
    lam,
    grad,
    mix,
    lse,
    qs,
    ks,
    vs,
    gain,
    dq,
    dkv,
    dkv_sib,
    sums,
    dk,
    dv,
):
    qb = query_rows(n)
    kb_rows = 2 * qb
    c = core[0]
    lambda_value = lam[0]
    dk[...] = jnp.zeros_like(dk)
    dv[...] = jnp.zeros_like(dv)
    sums[...] = jnp.zeros_like(sums)

    def block(j):
        at = pl.ds(pl.multiple_of(qb * j, qb), qb)
        pieces = []
        for i in range(qb // 32):
            run = order[j * (qb // 32) + i]
            b = pl.multiple_of(32 * lax.rem(run, 2), 32)
            pieces.append(grad[run // 2, pl.ds(b, 32), :])
        mixed_grad = jnp.concatenate(pieces, axis=0).astype(f32)
        mix_1, mix_2 = mix[0, at, :], mix[1, at, :]
        out = mix_1 - lambda_value * mix_2
        scale = rms_scale(out)
        sums[0:1, :] += jnp.sum(mixed_grad * out * scale, axis=0, keepdims=True) * (
            1.0 - lambda_init
        )
        heads_grad = rms_back(out, scale, gain[...], mixed_grad).astype(bf16)
        grad_f = heads_grad.astype(f32)
        dot_2 = grad_f * mix_2
        sums[1:2, :] += -jnp.sum(dot_2, axis=0, keepdims=True)
        delta_1 = jnp.sum(jnp.transpose(grad_f * mix_1), axis=0, keepdims=True)
        delta_2 = -lambda_value * jnp.sum(jnp.transpose(dot_2), axis=0, keepdims=True)
        q2 = two_maps(qs[at, :])
        lse_now = lse[j][0:1, :]

        def piece(kb, acc, diagonal):
            here = pl.ds(pl.multiple_of(kb_rows * kb, kb_rows), kb_rows)
            keys = ks[here, :]
            s = dot_nt(keys, q2) - lse_now
            if diagonal:
                col = lax.rem(lax.broadcasted_iota(jnp.int32, s.shape, 1), qb)
                allowed = (
                    lax.broadcasted_iota(jnp.int32, s.shape, 0)
                    <= 64 * (col // 32) + lax.rem(col, 32) + 32 * c
                )
                s = jnp.where(allowed, s, masked_score)
            prob = jnp.exp(s)
            prob_1, prob_2 = prob[:, :qb], prob[:, qb:]
            value_dot = dot_nt(vs[here, :], heads_grad)
            grads = jnp.concatenate(
                [
                    (prob_1 * (value_dot - delta_1)).astype(bf16),
                    (prob_2 * (-lambda_value * value_dot - delta_2)).astype(bf16),
                ],
                axis=1,
            )
            dv[here, :] += dot((prob_1 - lambda_value * prob_2).astype(bf16), heads_grad)
            dk[here, :] += dot(grads, q2)
            return acc + dot_tn(grads, keys)

        acc = lax.fori_loop(
            0, j, lambda kb, a: piece(kb, a, False), jnp.zeros((2 * qb, VW), f32)
        )
        acc = piece(j, acc, True)
        lane = lax.broadcasted_iota(jnp.int32, (qb, VW), 1)
        done = (jnp.where(lane < HALF, acc[:qb], acc[qb:]) * 0.125).astype(bf16)
        for i in range(qb // 32):
            run = order[j * (qb // 32) + i]
            b = pl.multiple_of(32 * lax.rem(run, 2), 32)
            dq[run // 2, pl.ds(b, 32), :] = done[32 * i : 32 * i + 32]

    loop(n * 64 // qb, block)

    def unsort(p):
        run = order[p]
        b = pl.multiple_of(32 * lax.rem(run, 2), 32)
        low = pl.multiple_of(64 * p + 32 * c, 32)
        high = pl.multiple_of(64 * p + 32 * (1 - c), 32)
        dkv[run // 2, pl.ds(b, 32), :VW] = dk[pl.ds(low, 32), :]
        dkv[run // 2, pl.ds(b, 32), VW:] = dv[pl.ds(low, 32), :]
        dkv_sib[run // 2, pl.ds(b, 32), :VW] = dk[pl.ds(high, 32), :]
        dkv_sib[run // 2, pl.ds(b, 32), VW:] = dv[pl.ds(high, 32), :]

    loop(2 * n, unsort)


def attend_back(place, order, core, lam, grad, saved, gain):
    n = place.n
    rows = 64 * n
    qb = query_rows(n)
    return pl.pallas_call(
        functools.partial(bwd_kernel, n),
        out_shape=[
            jax.ShapeDtypeStruct((n, 64, VW), bf16),
            jax.ShapeDtypeStruct((n, 64, 2 * VW), f32),
            jax.ShapeDtypeStruct((n, 64, 2 * VW), f32),
            jax.ShapeDtypeStruct((8, VW), f32),
        ],
        in_specs=[SMEM, SMEM, SMEM] + [VMEM] * 7,
        out_specs=[VMEM] * 4,
        scratch_shapes=[pltpu.VMEM((2 * rows, VW), f32)] * 2,
        compiler_params=pltpu.CompilerParams(vmem_limit_bytes=vmem_cap),
        cost_estimate=pl.CostEstimate(
            flops=30 * rows * rows * VW, bytes_accessed=30 * rows * VW, transcendentals=0
        ),
    )(order, core, lam, grad, *saved, gain)


def to_heads(rows):
    return rows.reshape(2, 2, 32, H, VW).transpose(3, 1, 0, 2, 4).reshape(H, 2, 64, VW)


def from_heads(blocks):
    lead = blocks.shape[:-4]
    k = len(lead)
    split = blocks.reshape(lead + (H, 2, 2, 32, VW))
    order = tuple(range(k)) + (k + 2, k + 1, k + 3, k, k + 4)
    return split.transpose(order).reshape(lead + (128, HW))


def body(
    place,
    inputs,
    positions,
    attn_gain,
    w_query,
    w_key,
    w_value,
    w_out,
    lambda_params,
    sub_gain,
    ffn_gain,
    w_gate,
    w_up,
    w_down,
    cotangent,
):
    n, tp, seq = place.n, place.tp, place.seq
    s, t, core, head, active = place.me()
    lin = s * tp + t
    row_count, width = inputs.shape
    part = width // n
    inputs_f = inputs.astype(f32)
    attn_scale = rms_scale(inputs_f)
    attn_normed = (inputs_f * attn_scale * attn_gain).astype(bf16)
    group_rows = lax.all_gather(
        jnp.concatenate([inputs, cotangent], axis=1), "tp", axis=0, tiled=True
    )
    inputs_all, cotangent_all = group_rows[:, :width], group_rows[:, width:]
    first_exp = jnp.exp(jnp.sum(lambda_params[0] * lambda_params[1]))
    second_exp = jnp.exp(jnp.sum(lambda_params[2] * lambda_params[3]))
    lambda_value = first_exp - second_exp + lambda_init
    lam = lambda_value.reshape(1)

    payload = jnp.concatenate(
        [to_heads(dot(attn_normed, w).astype(bf16)) for w in (w_query, w_key, w_value)], axis=3
    )
    own, sib, pos = send_heads(place, payload, positions.reshape(1, row_count), 1)
    blocks = pos.reshape(2 * n, 64)[:, 0] // 64
    run = jnp.arange(2 * n, dtype=jnp.int32)
    order = jnp.sum(jnp.where(blocks[None, :] == run[:, None], run[None, :], 0), axis=1)
    core_1 = core.reshape(1).astype(jnp.int32)
    head_gain = (sub_gain * (1.0 - lambda_init)).reshape(1, VW)
    mixed, *saved = attend(place, order, core_1, lam, own, sib, head_gain)
    normed_all = lax.all_gather(attn_normed, ("seq", "tp"), axis=0, tiled=True)
    mixed_all = from_heads(return_heads(place, mixed, 2)).reshape(tp * row_count, HW)

    middle_all = inputs_all.astype(f32) + dot(mixed_all, w_out)
    scale_all = rms_scale(middle_all)
    ffn_rows = (middle_all * scale_all * ffn_gain).astype(bf16)
    middle = lax.dynamic_slice_in_dim(middle_all, t * row_count, row_count, 0)
    ffn_scale = rms_scale(middle)
    gate_proj = dot(ffn_rows, w_gate)
    up_proj = dot(ffn_rows, w_up)
    gate_sig = jax.nn.sigmoid(gate_proj)
    gate_act = gate_proj * gate_sig
    hidden = (gate_act * up_proj).astype(bf16)
    hidden_grad = dot_nt(cotangent_all, w_down)
    gate_rows_grad = (
        hidden_grad * up_proj * gate_sig * (1.0 + gate_proj * (1.0 - gate_sig))
    ).astype(bf16)
    up_rows_grad = (hidden_grad * gate_act).astype(bf16)
    ffn_partial = dot_nt(gate_rows_grad, w_gate) + dot_nt(up_rows_grad, w_up)
    (grad_parts,) = moves(
        place,
        [Group(place, False)],
        [ffn_partial.astype(bf16).reshape(tp, row_count, width)],
        [(tp, row_count, width)],
        3,
    )
    own_partial = lax.dynamic_slice_in_dim(ffn_partial, t * row_count, row_count, 0)
    member = jnp.arange(tp)[:, None, None]
    ffn_in_grad = own_partial + jnp.sum(
        jnp.where(member == t, 0.0, grad_parts.astype(f32)), axis=0
    )
    ffn_gain_part = jnp.sum(ffn_in_grad * middle * ffn_scale, axis=0)
    middle_grad = cotangent.astype(f32) + rms_back(middle, ffn_scale, ffn_gain, ffn_in_grad)
    branch_grad = middle_grad.astype(bf16)

    down_part = dot_tn(cotangent_all, hidden).astype(bf16)
    gate_part = dot_tn(ffn_rows, gate_rows_grad).astype(bf16)
    up_part = dot_tn(ffn_rows, up_rows_grad).astype(bf16)

    def scatter_rows(array):
        return lax.psum_scatter(array, "seq", scatter_dimension=0, tiled=True)

    down_grad = scatter_rows(down_part).astype(f32).T
    gate_grad = scatter_rows(gate_part).astype(f32)
    up_grad = scatter_rows(up_part).astype(f32)

    mixed_grad = to_heads(dot_nt(branch_grad, w_out).astype(bf16))
    grad_heads, branch_all = moves(
        place,
        [Dispatch(place), Group(place, True)],
        [mixed_grad, branch_grad],
        [(n, 64, VW), (tp, row_count, width)],
        4,
    )
    mixed_cols = lax.dynamic_index_in_dim(
        mixed_all.reshape(tp * row_count, seq, tp, part), t, 2, keepdims=False
    ).reshape(tp * row_count, seq * part)
    out_part = dot_tn(mixed_cols, branch_all.reshape(tp * row_count, width)).astype(bf16)
    out_grad = scatter_rows(out_part).astype(f32)

    dq, dkv, dkv_sib, sums = attend_back(place, order, core_1, lam, grad_heads, saved, head_gain)
    swap = [(i, i ^ 1) for i in range(seq)]
    dkv = dkv + lax.ppermute(dkv_sib, "seq", swap)
    back = jnp.concatenate([dq, dkv.astype(bf16)], axis=2)

    ffn_out = dot(hidden, w_down)
    rows_back, out_parts = moves(
        place,
        [Collect(place), Group(place, False)],
        [back, ffn_out.astype(bf16).reshape(tp, row_count, width)],
        [(H, 2, 64, 3 * VW), (tp, row_count, width)],
        5,
    )
    output = (middle + jnp.sum(out_parts.astype(f32), axis=0)).astype(bf16)

    normed_half = lax.dynamic_index_in_dim(
        normed_all.reshape(n, 2, 2, 32, width), core, 2, keepdims=False
    ).reshape(n * 64, width)
    weight_part = dot_tn(normed_half, back.reshape(n * 64, 3 * VW))
    keep = lax.dynamic_slice_in_dim(weight_part, core * (width // 2), width // 2, 0)
    away = lax.dynamic_slice_in_dim(weight_part, (1 - core) * (width // 2), width // 2, 0)
    weight_half = (keep + lax.ppermute(away, "seq", swap)).astype(bf16)

    normed_grad = sum(
        dot_nt(from_heads(rows_back[..., i * VW : (i + 1) * VW]), w)
        for i, w in enumerate((w_query, w_key, w_value))
    )
    attn_gain_part = jnp.sum(normed_grad * inputs_f * attn_scale, axis=0)
    input_grad = middle_grad + rms_back(inputs_f, attn_scale, attn_gain, normed_grad)

    sums = jnp.where(active, sums, 0.0)
    pad = ((0, 0), (0, 128 - part))
    small = jnp.stack(
        [
            jnp.pad(attn_gain_part.reshape(n, part), pad),
            jnp.pad(ffn_gain_part.reshape(n, part), pad),
            jnp.broadcast_to(sums[0], (n, VW)),
            jnp.broadcast_to(sums[1], (n, VW)),
        ]
        + [jnp.zeros((n, VW), f32)] * 4,
        axis=1,
    )
    weight_rows, small_all = moves(
        place,
        [Collect(place, True), Everyone(place, False)],
        [weight_half.reshape(n // 2, part, 3 * VW), small],
        [(H, part, 3 * VW), (n, 8, VW)],
        6,
    )
    weight_rows = weight_rows.astype(f32).reshape(H, part, 3, VW).transpose(2, 1, 0, 3)
    weight_rows = weight_rows.reshape(3, part, HW)
    small_sum = jnp.sum(small_all, axis=0)
    lambda_total = jnp.sum(small_sum[3])
    lambda_grads = jnp.stack(
        [
            lambda_total * first_exp * lambda_params[1],
            lambda_total * first_exp * lambda_params[0],
            -lambda_total * second_exp * lambda_params[3],
            -lambda_total * second_exp * lambda_params[2],
        ]
    )
    lambda_norm = jnp.sqrt(jnp.sum(lambda_grads * lambda_grads))
    return (
        output,
        input_grad,
        small_sum[0, :part],
        weight_rows[0],
        weight_rows[1],
        weight_rows[2],
        out_grad,
        lambda_grads,
        small_sum[2],
        small_sum[1, :part],
        gate_grad,
        up_grad,
        down_grad,
        lambda_total,
        lambda_norm,
    )


def solution(mesh):
    place = Place(mesh.shape["seq"], mesh.shape["tp"])
    both = ("seq", "tp")
    placed = (
        P(both, None),
        P(both),
        P(),
        P(),
        P(),
        P(),
        P(),
        P(),
        P(),
        P(),
        P(None, "tp"),
        P(None, "tp"),
        P("tp", None),
        P(both, None),
    )
    return jax.shard_map(
        functools.partial(body, place),
        mesh=mesh,
        in_specs=placed,
        out_specs=(
            P(both, None),
            P(both, None),
            P(both),
            P(both, None),
            P(both, None),
            P(both, None),
            P(both, None),
            P(),
            P(),
            P(both),
            P("seq", "tp"),
            P("seq", "tp"),
            P("tp", "seq"),
            P(),
            P(),
        ),
        check_vma=False,
    )
```

time: 1420 us -> 528 us (0.37)
  waiting for transfers between devices: 584 us -> 29.2 us
  matrix products: 406 us -> 75.5 us
  Pallas kernels: 0 us -> 281 us
  blocking collectives: 184 us -> 0 us
  local copies, waits for them, and re-layouts: 138 us -> 74.5 us
  other arithmetic: 69.3 us -> 37 us
    reduce_scatter x7 -> x4, waiting for transfers between devices: 369 us -> 29.1 us  [scatter_rows(): return lax.psum_scatter(array, 'seq', scatter_dimension=0, tiled=True)]
    dot_general x77 -> x19, matrix products: 406 us -> 75.5 us  [the longest x7 29.3 us: dot(): return jnp.dot(left, right, preferred_element_type=f32)]
    pallas_call x0 -> x8, Pallas kernels: none -> 281 us  [the longest x4 126 us: moves(): pl.pallas_call(kernel, out_shape=[jax.ShapeDtypeStruct(s, a.dtype) for s,...]
    all_gather x2 -> x0, blocking collectives: 146 us -> none  [the longest x1 73.5 us: query_fold(): lax.all_gather(stats.astype(jnp.bfloat16), ('seq', 'tp'), axis=0, tiled=T...]
    all_gather x4 -> x2, waiting for transfers between devices: 127 us -> 0.01 us  [the longest x1 0.01 us: body(): lax.all_gather(jnp.concatenate([inputs, cotangent], axis=1), 'tp', axis=0...]
    slice x6 -> x5, local copies, waits for them, and re-layouts: 99.8 us -> 4.86 us  [the longest x2 3.18 us: body(): weight_rows[2]]
    psum x1 -> x0, waiting for transfers between devices: 87.5 us -> none  [tp_reduce(): lax.psum(partial_rows.astype(jnp.bfloat16), 'tp').astype(jnp.float32)]
    unnamed x1 -> x0, blocking collectives: 37.4 us -> none
  transfers between devices with their start and end apart: 12 -> 8, of which waited for: 7 -> 1; matrix products, arithmetic and copies ran while one was open for 26% -> 32% of each run, Pallas kernels for 0% -> 50%
where the time goes in v1:
time: 528 us; the launch traced here: 517 us
  Pallas kernels  281 us (53%)
  matrix products  75.5 us (14%)
  local copies, waits for them, and re-layouts  74.5 us (14%)
  other arithmetic  37 us (7%)
  waiting for transfers between devices  29.2 us (6%)
  between operations  19.6 us (4%)
    pallas_call x4, Pallas kernels, moves(): pl.pallas_call(kernel, out_shape=[jax.ShapeDtypeStruct(s, a.dtype) for s,...  126 us
    pallas_call x1, Pallas kernels, return_heads(): pl.pallas_call(kernel, out_shape=jax.ShapeDtypeStruct((place.tp, H, 2) +...  49.2 us
    pallas_call x1, Pallas kernels, send_heads(): pl.pallas_call(kernel, out_shape=[jax.ShapeDtypeStruct((n, rows, 3 * VW),...  37.1 us
    pallas_call x1, Pallas kernels, attend_back(): pl.pallas_call(functools.partial(bwd_kernel, n), out_shape=[jax.ShapeDtyp...  36.8 us
    pallas_call x1, Pallas kernels, attend(): pl.pallas_call(functools.partial(fwd_kernel, n), out_shape=[jax.ShapeDtyp...  32.6 us
    dot_general x7, matrix products, dot(): return jnp.dot(left, right, preferred_element_type=f32)  29.3 us
    reduce_scatter x4, waiting for transfers between devices, scatter_rows(): return lax.psum_scatter(array, 'seq', scatter_dimension=0, tiled=True)  29.1 us
    dot_general x7, matrix products, dot_nt(): lax.dot_general(left, right, (((1,), (1,)), ((), ())), preferred_element_...  23.6 us
  transfers between devices with their start and end apart: 8, of which 1 were waited for; matrix products, arithmetic and copies ran while one was open for 32% of the time, Pallas kernels for 50%

profile of v1, /device:TPU:0, one launch (start us, length us, event | category | flops | bytes accessed | tf_op | source)
XLA Modules:
  0.0 517.4 jit_solution(2880161112577884050)
XLA Ops:
  7.3 2.2 pad_maximum_fusion.2
  13.3 4.0 convolution_convert_fusion.6
  17.3 2.1 reshape.218
  19.3 1.9 copy.52
  21.3 4.2 convolution_convert_fusion.8
  25.5 2.1 reshape.214
  27.6 1.9 copy.50
  29.4 4.0 convolution_convert_fusion.7
  33.4 2.1 reshape.216
  36.7 2.4 pad_maximum_fusion.1.x
  39.0 37.1 %shard_map.253 = (bf16[32,64,384]{2,1,0:T(8,128)(2,1)}, bf16[32,64,256]{2,1,0:T(8,128)(2,1)}, s32[32,1,128]{2,1,0:T(1,128)}) custom-call(bf16[12,2,64,384]{3,2,1,0:T(8,128)(2,1)} %pad_maximum_fusion.1.x, s32[1,128]{1,0:T(1,128)} %bitcast.158), custom_call_target="tpu_custom_call" | custom-call | tf_op jit(solution)/shard_map/pallas_call | solution.py:361
  76.6 2.0 reduce.6
  78.6 1.4 reshape.221
  82.0 32.6 %shard_map.254 = (bf16[32,64,128]{2,1,0:T(8,128)(2,1)}, f32[2,2048,128]{2,1,0:T(8,128)}, f32[8,8,512]{2,1,0:T(8,128)}, bf16[2048,128]{1,0:T(8,128)(2,1)}, bf16[4...) custom-call(s32[64]{0:T(128)} %select_reduce_fusion.1.order, s32[1]{0:T(128)} %bitcast.8.core, f32[1]{0:T(128)} %bitcast.9.lam, ...), custom_call_target="tpu_custom_call" | custom-call | flops 6442450944 | bytes 3145728 | tf_op jit(solution)/shard_map/pallas_call | solution.py:495
  114.7 49.2 %shard_map.255 = bf16[4,12,2,64,128]{4,3,2,1,0:T(8,128)(2,1)} custom-call(bf16[32,64,128]{2,1,0:T(8,128)(2,1)} %get-tuple-element.37.x), custom_call_target="tpu_custom_call" | custom-call | tf_op jit(solution)/shard_map/pallas_call | solution.py:396
  163.9 3.9 copy.97
  167.7 9.6 %reshape_reshape_reshape.3 = bf16[512,8,4,48]{3,2,1,0:T(4,128)(2,1)} reshape(bf16[4,2,2,32,12,128]{5,4,3,2,1,0:T(8,128)(2,1)} %bitcast.126) | data formatting | bytes 3145728 | tf_op jit(solution)/shard_map/reshape;reshape;reshape | solution.py:749
  177.3 5.9 %constant_dynamic-slice_fusion = bf16[512,8,1,48]{3,2,1,0:T(2,128)(2,1)} fusion(bf16[512,8,4,48]{3,2,1,0:T(4,128)(2,1)} %reshape_reshape_reshape.3, s32[]{:T(128)S(6)} %select_n.58), kind=kLoop, calls=%fused_computation.71 | loop fusion | bytes 786436 | tf_op jit(solution)/shard_map/jit(dynamic_index_in_dim)/dynamic_slice | solution.py:748
  183.3 5.7 %copy.62 = bf16[512,8,1,48]{0,3,1,2:T(8,128)(2,1)} copy(bf16[512,8,1,48]{3,2,1,0:T(2,128)(2,1)} %constant_dynamic-slice_fusion) | data formatting | bytes 786432 | tf_op jit(solution)/shard_map/jit(dynamic_index_in_dim)/dynamic_slice | solution.py:748
  189.5 6.3 %multiply_reduce_fusion = (f32[512]{0:T(512)S(1)}, f32[512,1536]{1,0:T(8,128)S(1)}) fusion(bf16[1536,1536]{1,0:T(8,128)(2,1)} %param.20, bf16[64,8,12,128]{3,2,1,0:T(8,128)(2,1)} %bitcast.127, bf16[512,3072]{1,0:T(8,128)(2,1)} %all-gather.3.cloned.1.call-done), kind=kOutput, calls=%fused_computation.8 | convolution fusion | flops 2419064320 | bytes 11012096 | tf_op jit(solution)/shard_map/dot_general | solution.py:29
  196.3 1.3 copy-done.2
  197.5 1.4 copy-done.27
  198.9 1.8 fusion.26
  202.3 1.8 fusion.4
  204.2 3.6 multiply_convert_fusion.1
  207.8 1.8 fusion.27
  209.6 4.1 fusion.25
  213.7 31.6 %shard_map.256 = bf16[4,128,1536]{2,1,0:T(8,128)(2,1)} custom-call(bf16[4,128,1536]{2,1,0:T(8,128)(2,1)} %bitcast.148), custom_call_target="tpu_custom_call" | custom-call | tf_op jit(solution)/shard_map/pallas_call | solution.py:323
  245.5 2.1 select_reduce_fusion
  250.6 4.7 convolution_convert_fusion.5
  255.3 2.1 reshape.227
  257.4 1.9 copy.55
  259.3 29.0 %shard_map.257 = (bf16[32,64,128]{2,1,0:T(8,128)(2,1)}, bf16[4,128,1536]{2,1,0:T(8,128)(2,1)}) custom-call(bf16[12,2,64,128]{3,2,1,0:T(8,128)(2,1)} %bitcast.149, bf16[128,1536]{1,0:T(8,128)(2,1)} %copy-done.6), custom_call_target="tpu_custom_call" | custom-call | tf_op jit(solution)/shard_map/pallas_call | solution.py:323
  288.3 3.4 convolution_convert_fusion.4
  291.8 5.2 convolution_convert_fusion.2
  297.0 5.2 %convolution_convert_fusion.1 = bf16[1536,1024]{1,0:T(8,128)(2,1)} fusion(bf16[512,1536]{1,0:T(8,128)(2,1)} %copy-done.14, bf16[512,1024]{1,0:T(8,128)(2,1)} %copy-done.31), kind=kOutput, calls=%fused_computation.1 | convolution fusion | flops 1612185600 | bytes 5767168 | tf_op jit(solution)/shard_map/dot_general | solution.py:33
  302.3 36.8 %shard_map.258 = (bf16[32,64,128]{2,1,0:T(8,128)(2,1)}, f32[32,64,256]{2,1,0:T(8,128)}, f32[32,64,256]{2,1,0:T(8,128)}, f32[8,128]{1,0:T(8,128)}) custom-call(s32[64]{0:T(128)} %select_reduce_fusion.1.order, s32[1]{0:T(128)} %bitcast.8.core, f32[1]{0:T(128)} %bitcast.9.lam, bf16[32,64,128]{2,1,0:T(8,128)(2,1)} %get-tuple-element.38.grad, ...), custom_call_target="tpu_custom_call" | custom-call | flops 16106127360 | bytes 7864320 | tf_op jit(solution)/shard_map/pallas_call | solution.py:620
  339.1 5.3 %convolution_convert_fusion = bf16[1536,1024]{1,0:T(8,128)(2,1)} fusion(bf16[512,1024]{1,0:T(8,128)(2,1)} %get-tuple-element.63, bf16[512,3072]{1,0:T(8,128)(2,1)} %all-gather.3.cloned.1.call-done), kind=kOutput, calls=%fused_computation | convolution fusion | flops 1612185600 | bytes 5767168 | tf_op jit(solution)/shard_map/dot_general | solution.py:33
  345.8 1.3 pad.8
  348.3 5.3 %convolution_convert_fusion.3 = bf16[512,1536]{1,0:T(8,128)(2,1)} fusion(bf16[512,1024]{1,0:T(8,128)(2,1)} %get-tuple-element.63, bf16[1024,1536]{1,0:T(8,128)(2,1)} %param.26), kind=kOutput, calls=%fused_computation.9 | convolution fusion | flops 1611399168 | bytes 5767168 | tf_op jit(solution)/shard_map/dot_general | solution.py:29
  353.7 2.0 add_convert_fusion
  355.7 1.4 pad_maximum_fusion.refs_0_
  357.2 42.4 %shard_map.259 = (bf16[12,2,64,384]{3,2,1,0:T(8,128)(2,1)}, bf16[4,128,1536]{2,1,0:T(8,128)(2,1)}) custom-call(bf16[32,64,384]{2,1,0:T(8,128)(2,1)} %pad_maximum_fusion.refs_0_, bf16[4,128,1536]{2,1,0:T(8,128)(2,1)} %bitcast.147), custom_call_target="tpu_custom_call" | custom-call | tf_op jit(solution)/shard_map/pallas_call | solution.py:323
  399.6 1.5 fusion.24
  402.0 4.1 fusion.19
  406.1 4.0 convolution_add_fusion.3
  410.1 3.1 fusion.14
  413.9 1.3 pad.7
  415.2 1.3 stack_broadcast_in_dim.7
  416.5 1.3 stack_broadcast_in_dim.6
  418.4 1.7 stack.22.refs_1_
  420.1 2.6 convert_reduce_fusion
  422.7 3.7 constant_dynamic-slice_fusion.2
  426.4 3.5 fusion.28
  432.9 1.2 fusion.11
  434.1 1.8 convert_element_type.107
  435.9 2.0 convert_element_type.109
  437.9 2.0 convert_element_type.111
  439.9 29.1 %reduce-scatter.11.cloned.1.call-done = bf16[192,1024]{1,0:T(8,128)(2,1)} async-done(((bf16[1536,1024]{1,0:T(8,128)(2,1)}), bf16[192,1024]{1,0:T(8,128)(2,1)}) %reduce-scatter.11.cloned.1.call-update) | async-done | bytes 393232 | tf_op jit(solution)/shard_map/reduce_scatter | solution.py:734
  468.9 2.0 convert_bitcast_fusion
  470.9 2.2 add_convert_fusion.1
  473.1 22.6 %shard_map.260 = (bf16[12,48,384]{2,1,0:T(8,128)(2,1)}, f32[32,8,128]{2,1,0:T(8,128)}) custom-call(bf16[16,48,384]{2,1,0:T(8,128)(2,1)} %bitcast.133, f32[32,8,128]{2,1,0:T(8,128)} %stack.22.refs_1_), custom_call_target="tpu_custom_call" | custom-call | tf_op jit(solution)/shard_map/pallas_call | solution.py:323
  501.5 2.3 reshape.245
  503.8 3.1 fusion.23
  (129 shorter events, 25.5 us)
Async XLA Ops:
  7.2 197.0 %copy-start = (bf16[1536,1024]{1,0:T(8,128)(2,1)S(1)}, bf16[1536,1024]{1,0:T(8,128)(2,1)}, u32[]{:S(2)}) copy-start(bf16[1536,1024]{1,0:T(8,128)(2,1)} %param.25) | copy-start | bytes 9437188
  7.2 2.4 copy-start.4
  7.2 3.1 copy-start.18
  7.2 4.0 copy-start.20
  7.2 182.3 %all-gather.3.cloned.1.call-start = ((), (), s32[]{:S(2)}) async-start(), calls=%async_computation.4 | async-start | bytes 3932160 | tf_op jit(solution)/shard_map/all_gather | solution.py:675
  9.5 413.1 %all-gather.5.cloned.1.call-start = ((), (), s32[]{:S(2)}) async-start(), calls=%async_computation.5 | async-start | bytes 12976128 | tf_op jit(solution)/shard_map/all_gather | solution.py:694
  10.3 7.0 %copy-start.22 = (f32[128]{0:T(128)}, f32[128]{0:T(128)S(1)}, u32[]{:S(2)}) copy-start(f32[128]{0:T(128)S(1)} %get-tuple-element.85) | copy-start | bytes 1540
  11.2 422.9 %reduce-scatter.5.cloned.1.call-start = ((), (), s32[]{:S(2)}) async-start(), calls=%async_computation.6 | async-start | bytes 1327104 | tf_op jit(solution)/shard_map/reduce_scatter | solution.py:734
  35.5 46.0 %copy-start.30 = (f32[128]{0:T(128)S(1)}, f32[128]{0:T(128)}, u32[]{:S(2)}) copy-start(f32[128]{0:T(128)} %param.22) | copy-start | bytes 1540
  189.5 6.4 %copy-start.17 = (f32[1536]{0:T(1024)S(1)}, f32[1536]{0:T(1024)}, u32[]{:S(2)}) copy-start(f32[1536]{0:T(1024)} %param.23) | copy-start | bytes 18436
  195.9 1.6 copy-start.2
  195.9 3.0 copy-start.27
  198.9 5.2 %copy-start.14 = (bf16[512,1536]{1,0:T(8,128)(2,1)}, bf16[512,1536]{1,0:T(8,128)(2,1)S(1)}, u32[]{:S(2)}) copy-start(bf16[512,1536]{1,0:T(8,128)(2,1)S(1)} %multiply_convert_fusion) | copy-start | bytes 4718596
  198.9 2.5 copy-start.28
  198.9 3.4 copy-start.29
  207.8 1.8 copy-start.32
  207.8 1.8 copy-start.31
  213.7 31.6 %copy-start.3 = (f32[512,1536]{1,0:T(8,128)S(1)}, f32[512,1536]{1,0:T(8,128)}, u32[]{:S(2)}) copy-start(f32[512,1536]{1,0:T(8,128)} %copy-done.2) | copy-start | bytes 9437188
  245.4 2.4 copy-start.15
  245.5 3.1 copy-start.13
  249.8 0.8 copy-start.6
  291.7 144.2 %reduce-scatter.7.cloned.1.call-start = ((), (), s32[]{:S(2)}) async-start(), calls=%async_computation.7 | async-start | bytes 3538944 | tf_op jit(solution)/shard_map/reduce_scatter | solution.py:734
  296.9 141.0 %reduce-scatter.9.cloned.1.call-start = ((), (), s32[]{:S(2)}) async-start(), calls=%async_computation.8 | async-start | bytes 3538944 | tf_op jit(solution)/shard_map/reduce_scatter | solution.py:734
  302.3 166.7 %reduce-scatter.11.cloned.1.call-start = ((), (), s32[]{:S(2)}) async-start(), calls=%async_computation.9 | async-start | bytes 3538944 | tf_op jit(solution)/shard_map/reduce_scatter | solution.py:734
  339.1 14.6 %collective-permute-start = (f32[32,64,256]{2,1,0:T(8,128)}, f32[32,64,256]{2,1,0:T(8,128)}, u32[]{:S(2)}, u32[]{:S(2)}) collective-permute-start(f32[32,64,256]{2,1,0:T(8,128)} %get-tuple-element.46), channel_id=1, source_target_pairs={{0,4},{4,0},{8,12},{12,8},{16,20},{20,16},{24,28},{28,24},{1,5},{5... | collective-permute-start | bytes 6291464 | tf_op jit(solution)/shard_map/ppermute | solution.py:756
  344.4 0.7 copy-start.19
  348.3 5.4 %copy-start.12 = (f32[32,64,256]{2,1,0:T(8,128)S(1)}, f32[32,64,256]{2,1,0:T(8,128)}, u32[]{:S(2)}) copy-start(f32[32,64,256]{2,1,0:T(8,128)} %get-tuple-element.45) | copy-start | bytes 6291460
  353.7 2.0 copy-start.16
  399.6 10.4 %slice-start = ((s8[4718592]{0:T(1024)(128)(4,1)}), s8[4194304]{0:T(1024)(128)(4,1)S(1)}, s32[]{:S(2)}) async-start(s8[4718592]{0:T(1024)(128)(4,1)} %bitcast.124), calls=%async_computation.10 | async-start | bytes 8388608
  401.9 8.1 %slice-start.1 = ((s8[4718592]{0:T(1024)(128)(4,1)}), s8[524288]{0:T(1024)(128)(4,1)S(1)}, s32[]{:S(2)}) async-start(s8[4718592]{0:T(1024)(128)(4,1)} %bitcast.124), calls=%async_computation.11 | async-start | bytes 1048576
  406.1 4.0 copy-start.23
  413.9 8.8 %copy-start.26 = (f32[128]{0:T(128)S(1)}, f32[128]{0:T(128)}, u32[]{:S(2)}) copy-start(f32[128]{0:T(128)} %get-tuple-element.56) | copy-start | bytes 1540
  422.7 3.7 copy-start.5
  429.9 2.5 copy-start.10
  429.9 1.7 copy-start.8
  429.9 2.5 copy-start.7
  429.9 3.0 copy-start.9
  429.9 3.0 copy-start.24
  429.9 3.0 copy-start.25
  431.1 39.8 %collective-permute-start.1 = (f32[768,384]{1,0:T(8,128)}, f32[768,384]{1,0:T(8,128)}, u32[]{:S(2)}, u32[]{:S(2)}) collective-permute-start(f32[768,384]{1,0:T(8,128)} %constant_dynamic-slice_fusion.1), channel_id=1, source_target_pairs={{0,4},{4,0},{8,12},{12,8},{16,20},{20,16},{24,28},{28,24},{1,5},{5... | collective-permute-start | bytes 3538952 | tf_op jit(solution)/shard_map/ppermute | solution.py:775
  434.1 36.8 %copy-start.11 = (f32[1536,384]{1,0:T(8,128)S(1)}, f32[1536,384]{1,0:T(8,128)}, u32[]{:S(2)}) copy-start(f32[1536,384]{1,0:T(8,128)} %copy-done.10) | copy-start | bytes 7077892
  439.9 59.7 %copy-start.21 = (f32[4,64]{1,0:T(4,128)S(1)}, f32[4,64]{1,0:T(4,128)}, u32[]{:S(2)}) copy-start(f32[4,64]{1,0:T(4,128)} %param.21) | copy-start | bytes 3076
  503.8 5.2 %copy-start.1 = (bf16[1536,1024]{1,0:T(8,128)(2,1)S(1)}, bf16[1536,1024]{1,0:T(8,128)(2,1)}, u32[]{:S(2)}) copy-start(bf16[1536,1024]{1,0:T(8,128)(2,1)} %param.25) | copy-start | bytes 9437188
Sparse Core Ops, SparseCore 0:
  10.5 64.0 all-gather.2
  78.1 117.6 all-gather.4
  291.8 30.5 reduce-scatter.4
  324.6 38.8 reduce-scatter.6
  365.6 59.6 reduce-scatter.8
  427.4 41.4 reduce-scatter.10

commit v2 on v1

--- a/solution.py
+++ b/solution.py
@@ -67,6 +67,12 @@
         return linear // self.tp, lax.rem(linear, self.tp)
 
 
+def busy(microseconds):
+    return pl.CostEstimate(
+        flops=int(microseconds * 1e9), bytes_accessed=int(microseconds * 3e6), transcendentals=0
+    )
+
+
 def remote(src, dst, send, recv, where):
     return pltpu.make_async_remote_copy(
         src_ref=src, dst_ref=dst, send_sem=send, recv_sem=recv, device_id=where, device_id_type=MESH
@@ -82,37 +88,30 @@
 
 
 class Dispatch:
-    def __init__(self, place):
-        self.p = place
+    def __init__(self, place, cut):
+        self.p, self.cut = place, cut
         self.sems = [2 * H, place.n, 1]
 
-    def start(self, x, o, send, recv, here):
+    def start_one(self, index, x, o, send, recv, here):
         p = self.p
         s, t, c, head, active = p.me()
         lin = s * p.tp + t
-
-        def step(k):
-            index = lax.rem(k + lin, 2 * H)
-            ds, dt = p.head_device(index)
-            mine = jnp.logical_and(ds == s, dt == t)
-
-            @pl.when(jnp.logical_not(mine))
-            def _():
-                remote(
-                    x.at[index // 2, lax.rem(index, 2)],
-                    o.at[lin],
-                    send.at[index],
-                    recv.at[lin],
-                    (ds, dt),
-                ).start()
-
-            @pl.when(mine)
-            def _():
-                pltpu.make_async_copy(
-                    x.at[index // 2, lax.rem(index, 2)], o.at[lin], here.at[0]
-                ).start()
-
-        loop(2 * H, step)
+        ds, dt = p.head_device(index)
+        mine = jnp.logical_and(ds == s, dt == t)
+        source = self.cut(x, index // 2, lax.rem(index, 2))
+
+        @pl.when(jnp.logical_not(mine))
+        def _():
+            remote(source, o.at[lin], send.at[index], recv.at[lin], (ds, dt)).start()
+
+        @pl.when(mine)
+        def _():
+            pltpu.make_async_copy(source, o.at[lin], here.at[0]).start()
+
+    def start(self, *refs):
+        p = self.p
+        lin = lax.axis_index("seq") * p.tp + lax.axis_index("tp")
+        loop(2 * H, lambda k: self.start_one(lax.rem(k + lin, 2 * H), *refs))
 
     def finish(self, x, o, send, recv, here, arrived=None):
         p = self.p
@@ -121,7 +120,7 @@
 
         @pl.when(active)
         def _():
-            pltpu.make_async_copy(x.at[0, 0], o.at[lin], here.at[0]).wait()
+            pltpu.make_async_copy(self.cut(x, head, c), o.at[lin], here.at[0]).wait()
             if arrived is not None:
                 arrived(lin)
 
@@ -139,17 +138,15 @@
             @pl.when(jnp.logical_not(jnp.logical_and(ds == s, dt == t)))
             def _():
                 remote(
-                    x.at[k // 2, lax.rem(k, 2)], o.at[0], send.at[k], recv.at[0], (ds, dt)
+                    self.cut(x, k // 2, lax.rem(k, 2)), o.at[0], send.at[k], recv.at[0], (ds, dt)
                 ).wait_send()
 
         loop(2 * H, sent)
 
 
 class Collect:
-    def __init__(self, place, halves=False, grouped=False):
-        self.p = place
-        self.halves = halves
-        self.grouped = grouped
+    def __init__(self, place, into, halves=False):
+        self.p, self.into, self.halves = place, into, halves
         self.sems = [place.n, 2 * H, 1]
 
     def start(self, x, o, send, recv, here):
@@ -163,8 +160,7 @@
             def step(k):
                 slot = lax.rem(k + lin, count)
                 other = slot + c * count if self.halves else slot
-                into = o.at[lax.rem(other, p.tp)] if self.grouped else o
-                into = into.at[head] if self.halves else into.at[head, c]
+                into = self.into(o, lax.rem(other, p.tp), head, c)
 
                 @pl.when(other != lin)
                 def _():
@@ -178,33 +174,30 @@
 
             loop(count, step)
 
-    def finish(self, x, o, send, recv, here):
+    def got(self, index, x, o, send, recv, here):
+        p = self.p
+        s, t = lax.axis_index("seq"), lax.axis_index("tp")
+        into = self.into(o, t, index // 2, lax.rem(index, 2))
+        ds, dt = p.head_device(index)
+        mine = jnp.logical_and(ds == s, dt == t)
+
+        @pl.when(jnp.logical_not(mine))
+        def _():
+            remote(into, into, send.at[0], recv.at[index], (s, t)).wait_recv()
+
+        @pl.when(mine)
+        def _():
+            pltpu.make_async_copy(x.at[0], into, here.at[0]).wait()
+
+    def sent(self, x, o, send, recv, here):
         p = self.p
         s, t, c, head, active = p.me()
         lin = s * p.tp + t
         count = p.n // 2 if self.halves else p.n
-        half = lin // count if self.halves else 0
-        o = o.at[t] if self.grouped else o
-
-        def got(k):
-            index = 2 * k + half if self.halves else k
-            into = o.at[k] if self.halves else o.at[k // 2, lax.rem(k, 2)]
-            ds, dt = p.head_device(index)
-            mine = jnp.logical_and(ds == s, dt == t)
-
-            @pl.when(jnp.logical_not(mine))
-            def _():
-                remote(into, into, send.at[0], recv.at[index], (s, t)).wait_recv()
-
-            @pl.when(mine)
-            def _():
-                pltpu.make_async_copy(x.at[0], into, here.at[0]).wait()
-
-        loop(H if self.halves else 2 * H, got)
 
         @pl.when(active)
         def _():
-            def sent(k):
+            def one(k):
                 other = k + c * count if self.halves else k
 
                 @pl.when(other != lin)
@@ -213,7 +206,17 @@
                         x.at[k], x.at[k], send.at[k], recv.at[0], p.device(other)
                     ).wait_send()
 
-            loop(count, sent)
+            loop(count, one)
+
+    def finish(self, *refs):
+        p = self.p
+        if self.halves:
+            lin = lax.axis_index("seq") * p.tp + lax.axis_index("tp")
+            half = lin // (p.n // 2)
+            loop(H, lambda k: self.got(2 * k + half, *refs))
+        else:
+            loop(2 * H, lambda k: self.got(k, *refs))
+        self.sent(*refs)
 
 
 class Everyone:
@@ -309,98 +312,286 @@
     pl.semaphore_wait(barrier, place.n - 1)
 
 
-def moves(place, parts, arrays, shapes, ident, cost=0):
-    count = len(parts)
+def moves(place, parts, arrays, outs, ident, cost, work=None, operands=(), results=(), scratch=()):
+    count, extra = len(parts), len(operands)
 
     def kernel(*refs):
-        ins, outs, sems = refs[:count], refs[count : 2 * count], refs[2 * count :]
+        ins, given = refs[:count], refs[count : count + extra]
+        refs = refs[count + extra :]
+        into, made = refs[:count], refs[count : count + len(results)]
+        refs = refs[count + len(results) :]
+        sems, rest = refs[: 3 * count], refs[3 * count :]
         greet(place)
         for i, part in enumerate(parts):
-            part.start(ins[i], outs[i], *sems[3 * i : 3 * i + 3])
+            part.start(ins[i], into[i], *sems[3 * i : 3 * i + 3])
+        if work is not None:
+            work(given, made, rest)
         for i, part in enumerate(parts):
-            part.finish(ins[i], outs[i], *sems[3 * i : 3 * i + 3])
+            part.finish(ins[i], into[i], *sems[3 * i : 3 * i + 3])
 
     return pl.pallas_call(
         kernel,
-        out_shape=[jax.ShapeDtypeStruct(s, a.dtype) for s, a in zip(shapes, arrays)],
-        in_specs=[ANY] * count,
-        out_specs=[ANY] * count,
-        scratch_shapes=[pltpu.SemaphoreType.DMA((k,)) for part in parts for k in part.sems],
+        out_shape=[jax.ShapeDtypeStruct(s, a.dtype) for s, a in zip(outs, arrays)]
+        + [shape for shape, spec in results],
+        in_specs=[ANY] * count + [spec for array, spec in operands],
+        out_specs=[ANY] * count + [spec for shape, spec in results],
+        scratch_shapes=[pltpu.SemaphoreType.DMA((k,)) for part in parts for k in part.sems]
+        + list(scratch),
+        compiler_params=pltpu.CompilerParams(
+            collective_id=ident, has_side_effects=True, vmem_limit_bytes=vmem_cap
+        ),
+        cost_estimate=busy(cost),
+    )(*arrays, *[array for array, spec in operands])
+
+
+def send_heads(place, normed, weights, run_pos, cotangent, ident):
+    n, rows = place.n, normed.shape[0] // 2
+    width = normed.shape[1]
+    give = Dispatch(place, lambda x, h, c: x.at[h, c])
+    tell = Everyone(place, True)
+    share = Group(place, True)
+
+    def turn(k):
+        lin = lax.axis_index("seq") * place.tp + lax.axis_index("tp")
+        return lax.rem(k + lin, H)
+
+    def kernel(x, wq, wk, wv, r, cot, own, sib, pos, cot_all, made, *sems):
+        s, t, c, head, active = place.me()
+        send, recv = sems[9], sems[10]
+        k = pl.program_id(0)
+
+        @pl.when(k == 0)
+        def _():
+            greet(place)
+            tell.start(r, pos, *sems[3:6])
+            share.start(cot, cot_all, *sems[6:9])
+
+        now = turn(k)
+        for i, w in enumerate((wq, wk, wv)):
+            out = dot(x[...], w[...]).astype(bf16)
+            made[now, 0, :, i * VW : (i + 1) * VW] = out[:rows]
+            made[now, 1, :, i * VW : (i + 1) * VW] = out[rows:]
+        give.start_one(2 * now, made, own, *sems[:3])
+        give.start_one(2 * now + 1, made, own, *sems[:3])
+
+        @pl.when(k == H - 1)
+        def _():
+            def pass_on(j):
+                return remote(
+                    own.at[j, :, VW : 3 * VW],
+                    sib.at[j],
+                    send.at[j],
+                    recv.at[j],
+                    (s + 1 - 2 * c, t),
+                )
+
+            give.finish(made, own, *sems[:3], arrived=lambda j: pass_on(j).start())
+
+            @pl.when(active)
+            def _():
+                def done(j):
+                    pass_on(j).wait_recv()
+                    pass_on(j).wait_send()
+
+                loop(n, done)
+
+            tell.finish(r, pos, *sems[3:6])
+            share.finish(cot, cot_all, *sems[6:9])
+
+    columns = pl.BlockSpec((width, VW), lambda k: (0, turn(k)))
+    return pl.pallas_call(
+        kernel,
+        grid=(H,),
+        out_shape=[
+            jax.ShapeDtypeStruct((n, rows, 3 * VW), bf16),
+            jax.ShapeDtypeStruct((n, rows, 2 * VW), bf16),
+            jax.ShapeDtypeStruct((n,) + run_pos.shape, run_pos.dtype),
+            jax.ShapeDtypeStruct((place.tp,) + cotangent.shape, bf16),
+        ],
+        in_specs=[pl.BlockSpec(normed.shape, lambda k: (0, 0))] + [columns] * 3 + [ANY] * 2,
+        out_specs=[ANY] * 4,
+        scratch_shapes=[pltpu.VMEM((H, 2, rows, 3 * VW), bf16)]
+        + [pltpu.SemaphoreType.DMA((k,)) for k in give.sems + tell.sems + share.sems + [n, n]],
+        compiler_params=pltpu.CompilerParams(
+            collective_id=ident, has_side_effects=True, vmem_limit_bytes=vmem_cap
+        ),
+        cost_estimate=busy(35),
+    )(normed, *weights, run_pos, cotangent)
+
+
+def return_heads(place, mixed, ident):
+    n, rows = place.n, mixed.shape[1]
+
+    def into(o, t, h, c):
+        return o.at[
+            t,
+            pl.ds(pl.multiple_of(rows * c, rows), rows),
+            pl.ds(pl.multiple_of(VW * h, VW), VW),
+        ]
+
+    back = Collect(place, into)
+
+    def kernel(x, o, *sems):
+        s, t = lax.axis_index("seq"), lax.axis_index("tp")
+        greet(place)
+        back.start(x, o, *sems[:3])
+        send, recv = sems[3], sems[4]
+
+        def share(k, c, slot):
+            other = lax.rem(t + k, place.tp)
+            return remote(
+                o.at[t, rows * c : rows * c + rows, :],
+                o.at[slot(other), rows * c : rows * c + rows, :],
+                send.at[2 * other + c],
+                recv.at[2 * slot(other) + c],
+                (s, other),
+            )
+
+        for c in range(2):
+            loop(H, lambda h: back.got(2 * h + c, x, o, *sems[:3]))
+            for k in range(1, place.tp):
+                share(k, c, lambda other: t).start()
+        for c in range(2):
+            for k in range(1, place.tp):
+                both = share(k, c, lambda other: other)
+                both.wait_recv()
+                both.wait_send()
+        back.sent(x, o, *sems[:3])
+
+    return pl.pallas_call(
+        kernel,
+        out_shape=jax.ShapeDtypeStruct((place.tp, 2 * rows, HW), mixed.dtype),
+        in_specs=[ANY],
+        out_specs=ANY,
+        scratch_shapes=[
+            pltpu.SemaphoreType.DMA((k,)) for k in back.sems + [2 * place.tp, 2 * place.tp]
+        ],
         compiler_params=pltpu.CompilerParams(collective_id=ident, has_side_effects=True),
-    )(*arrays)
-
-
-def send_heads(place, payload, run_pos, ident):
-    n, rows = place.n, payload.shape[2]
-    give, tell = Dispatch(place), Everyone(place, True)
-
-    def kernel(x, r, own, sib, pos, *sems):
-        s, t, c, head, active = place.me()
-        send, recv = sems[6], sems[7]
+        cost_estimate=busy(35),
+    )(mixed)
+
+
+def finish_heads(
+    place, dq, dkv, dkv_sib, rows_all, gain, weights, ffn_out, branch_grad, ident
+):
+    n, half = place.n, dq.shape[1]
+    width = rows_all.shape[2]
+    part, chunk, lot = width // n, 256, 8
+
+    def into(o, t, h, c):
+        return o.at[
+            pl.ds(pl.multiple_of(half * c, half), half),
+            pl.ds(pl.multiple_of(3 * VW * h, 3 * VW), 3 * VW),
+        ]
+
+    back, ffn, share = Collect(place, into), Group(place, False), Group(place, True)
+
+    def kernel(*refs):
+        dq, dkv, dkv_sib, rows_all, gain, *refs = refs
+        weights, refs = refs[:3], refs[3:]
+        ffn_out, branch, normed_grad, weight_half, ffn_parts, branch_all, *refs = refs
+        other_dkv, grads, rows_back, raw, held, away, other, w_all, *sems = refs
+        s, t = lax.axis_index("seq"), lax.axis_index("tp")
+        c = lax.rem(s, 2)
+        send, recv, raw_sem, w_sem = sems[9:]
+        sibling = (s + 1 - 2 * c, t)
         greet(place)
-        give.start(x, own, *sems[:3])
-        tell.start(r, pos, *sems[3:6])
-
-        def pass_on(k):
-            return remote(
-                own.at[k, :, VW : 3 * VW], sib.at[k], send.at[k], recv.at[k], (s + 1 - 2 * c, t)
+        swap = remote(dkv_sib, other_dkv, send.at[0], recv.at[0], sibling)
+        swap.start()
+
+        def fetch(i):
+            return pltpu.make_async_copy(
+                rows_all.at[
+                    pl.ds(lot * i, lot), pl.ds(pl.multiple_of(half * c, half), half), :
+                ],
+                raw.at[lax.rem(i, 2)],
+                raw_sem.at[lax.rem(i, 2)],
             )
 
-        give.finish(x, own, *sems[:3], arrived=lambda k: pass_on(k).start())
-
-        @pl.when(active)
-        def _():
-            def done(k):
-                pass_on(k).wait_recv()
-                pass_on(k).wait_send()
-
-            loop(n, done)
-
-        tell.finish(r, pos, *sems[3:6])
+        fetch(0).start()
+        loads = [
+            pltpu.make_async_copy(w, w_all.at[i], w_sem.at[i]) for i, w in enumerate(weights)
+        ]
+        for load in loads:
+            load.start()
+        swap.wait_recv()
+
+        def join(i):
+            grads[i, :, :VW] = dq[i]
+            grads[i, :, VW:] = (dkv[i] + other_dkv[i].astype(f32)).astype(bf16)
+
+        loop(n, join)
+        back.start(grads, rows_back, *sems[:3])
+        share.start(branch, branch_all, *sems[6:9])
+        ffn.start(ffn_out, ffn_parts, *sems[3:6])
+        held[...] = jnp.zeros_like(held)
+
+        def rows(i):
+            @pl.when(i + 1 < n // lot)
+            def _():
+                fetch(i + 1).start()
+
+            fetch(i).wait()
+            x = raw[lax.rem(i, 2)].reshape(lot * half, width).astype(f32)
+            x = (x * rms_scale(x) * gain[...]).astype(bf16)
+            g = grads[pl.ds(lot * i, lot)].reshape(lot * half, 3 * VW)
+            for k in range(width // chunk):
+                held[k * chunk : (k + 1) * chunk, :] += dot_tn(
+                    x[:, k * chunk : (k + 1) * chunk], g
+                )
+
+        loop(n // lot, rows)
+        low = pl.multiple_of(c * (width // 2), width // 2)
+        high = pl.multiple_of((1 - c) * (width // 2), width // 2)
+        away[...] = held[pl.ds(high, width // 2), :].astype(bf16)
+        cross = remote(away, other, send.at[1], recv.at[1], sibling)
+        cross.start()
+        back.finish(grads, rows_back, *sems[:3])
+        for load in loads:
+            load.wait()
+        total = None
+        for h in range(0, H, 2):
+            for i in range(3):
+                at = (3 * h + i) * VW
+                x = jnp.concatenate(
+                    [rows_back[:, at : at + VW], rows_back[:, at + 3 * VW : at + 4 * VW]], axis=1
+                )
+                new = dot_nt(x, w_all[i, :, h * VW : (h + 2) * VW])
+                total = new if total is None else total + new
+        normed_grad[...] = total
+        cross.wait_recv()
+        weight_half[...] = (held[pl.ds(low, width // 2), :] + other[...].astype(f32)).astype(bf16)
+        share.finish(branch, branch_all, *sems[6:9])
+        ffn.finish(ffn_out, ffn_parts, *sems[3:6])
+        swap.wait_send()
+        cross.wait_send()
 
     return pl.pallas_call(
         kernel,
         out_shape=[
-            jax.ShapeDtypeStruct((n, rows, 3 * VW), payload.dtype),
-            jax.ShapeDtypeStruct((n, rows, 2 * VW), payload.dtype),
-            jax.ShapeDtypeStruct((n,) + run_pos.shape, run_pos.dtype),
+            jax.ShapeDtypeStruct((2 * half, width), f32),
+            jax.ShapeDtypeStruct((width // 2, 3 * VW), bf16),
+            jax.ShapeDtypeStruct(ffn_out.shape, bf16),
+            jax.ShapeDtypeStruct((place.tp,) + branch_grad.shape, bf16),
         ],
-        in_specs=[ANY] * 2,
-        out_specs=[ANY] * 3,
-        scratch_shapes=[pltpu.SemaphoreType.DMA((k,)) for k in give.sems + tell.sems + [n, n]],
-        compiler_params=pltpu.CompilerParams(collective_id=ident, has_side_effects=True),
-    )(payload, run_pos)
-
-
-def return_heads(place, mixed, ident):
-    n = place.n
-    back, share = Collect(place, grouped=True), Group(place, True)
-
-    def kernel(x, o, *sems):
-        t = lax.axis_index("tp")
-        s = lax.axis_index("seq")
-        greet(place)
-        own = o.at[t]
-        back.start(x, o, *sems[:3])
-        back.finish(x, o, *sems[:3])
-        send, recv = sems[3], sems[4]
-        for k in range(1, place.tp):
-            other = lax.rem(t + k, place.tp)
-            remote(own, o.at[t], send.at[other], recv.at[t], (s, other)).start()
-        for k in range(1, place.tp):
-            other = lax.rem(t + k, place.tp)
-            both = remote(own, o.at[other], send.at[other], recv.at[other], (s, other))
-            both.wait_recv()
-            both.wait_send()
-
-    return pl.pallas_call(
-        kernel,
-        out_shape=jax.ShapeDtypeStruct((place.tp, H, 2) + mixed.shape[1:], mixed.dtype),
-        in_specs=[ANY],
-        out_specs=ANY,
-        scratch_shapes=[pltpu.SemaphoreType.DMA((k,)) for k in back.sems + share.sems[:2]],
-        compiler_params=pltpu.CompilerParams(collective_id=ident, has_side_effects=True),
-    )(mixed)
+        in_specs=[VMEM, VMEM, ANY, ANY, VMEM] + [ANY] * 5,
+        out_specs=[VMEM, VMEM, ANY, ANY],
+        scratch_shapes=[
+            pltpu.VMEM((n, half, 2 * VW), bf16),
+            pltpu.VMEM((n, half, 3 * VW), bf16),
+            pltpu.VMEM((2 * half, 3 * HW), bf16),
+            pltpu.VMEM((2, lot, half, width), bf16),
+            pltpu.VMEM((width, 3 * VW), f32),
+            pltpu.VMEM((width // 2, 3 * VW), bf16),
+            pltpu.VMEM((width // 2, 3 * VW), bf16),
+            pltpu.VMEM((3,) + weights[0].shape, bf16),
+        ]
+        + [pltpu.SemaphoreType.DMA((k,)) for k in back.sems + ffn.sems + share.sems + [2, 2, 2, 3]],
+        compiler_params=pltpu.CompilerParams(
+            collective_id=ident, has_side_effects=True, vmem_limit_bytes=vmem_cap
+        ),
+        cost_estimate=busy(40),
+    )(dq, dkv, dkv_sib, rows_all, gain, *weights, ffn_out, branch_grad)
 
 
 def query_rows(n):
@@ -415,10 +606,15 @@
     )
 
 
-def fwd_kernel(n, order, core, lam, own, sib, gain, mixed, mix, lse, qs, ks, vs, score):
+def fwd_kernel(n, pos, lam, own, sib, gain, mixed, mix, lse, qs, ks, vs, order, score):
     qb = query_rows(n)
     kb_rows = 2 * qb
-    c = core[0]
+    c = lax.rem(lax.axis_index("seq"), 2)
+
+    def place_run(run):
+        order[pos[run // 2, lax.rem(run, 2) * 64] // 64] = run
+
+    loop(2 * n, place_run)
     lambda_value = lam[0]
 
     def sort(p):
@@ -488,7 +684,7 @@
     loop(n * 64 // qb, block)
 
 
-def attend(place, order, core, lam, own, sib, gain):
+def attend(place, pos, lam, own, sib, gain):
     n = place.n
     rows = 64 * n
     qb = query_rows(n)
@@ -501,21 +697,18 @@
             jax.ShapeDtypeStruct((rows, VW), bf16),
             jax.ShapeDtypeStruct((2 * rows, VW), bf16),
             jax.ShapeDtypeStruct((2 * rows, VW), bf16),
+            jax.ShapeDtypeStruct((2 * n,), jnp.int32),
         ],
-        in_specs=[SMEM, SMEM, SMEM, VMEM, VMEM, VMEM],
-        out_specs=[VMEM] * 6,
+        in_specs=[SMEM, SMEM, VMEM, VMEM, VMEM],
+        out_specs=[VMEM] * 6 + [SMEM],
         scratch_shapes=[pltpu.VMEM((2 * qb, 2 * rows), f32)],
         compiler_params=pltpu.CompilerParams(vmem_limit_bytes=vmem_cap),
-        cost_estimate=pl.CostEstimate(
-            flops=12 * rows * rows * VW, bytes_accessed=12 * rows * VW, transcendentals=0
-        ),
-    )(order, core, lam, own, sib, gain)
+        cost_estimate=busy(30),
+    )(pos, lam, own, sib, gain)
 
 
 def bwd_kernel(
     n,
-    order,
-    core,
     lam,
     grad,
     mix,
@@ -523,6 +716,7 @@
     qs,
     ks,
     vs,
+    order,
     gain,
     dq,
     dkv,
@@ -533,7 +727,7 @@
 ):
     qb = query_rows(n)
     kb_rows = 2 * qb
-    c = core[0]
+    c = lax.rem(lax.axis_index("seq"), 2)
     lambda_value = lam[0]
     dk[...] = jnp.zeros_like(dk)
     dv[...] = jnp.zeros_like(dv)
@@ -607,13 +801,13 @@
         high = pl.multiple_of(64 * p + 32 * (1 - c), 32)
         dkv[run // 2, pl.ds(b, 32), :VW] = dk[pl.ds(low, 32), :]
         dkv[run // 2, pl.ds(b, 32), VW:] = dv[pl.ds(low, 32), :]
-        dkv_sib[run // 2, pl.ds(b, 32), :VW] = dk[pl.ds(high, 32), :]
-        dkv_sib[run // 2, pl.ds(b, 32), VW:] = dv[pl.ds(high, 32), :]
+        dkv_sib[run // 2, pl.ds(b, 32), :VW] = dk[pl.ds(high, 32), :].astype(bf16)
+        dkv_sib[run // 2, pl.ds(b, 32), VW:] = dv[pl.ds(high, 32), :].astype(bf16)
 
     loop(2 * n, unsort)
 
 
-def attend_back(place, order, core, lam, grad, saved, gain):
+def attend_back(place, lam, grad, saved, gain):
     n = place.n
     rows = 64 * n
     qb = query_rows(n)
@@ -622,29 +816,20 @@
         out_shape=[
             jax.ShapeDtypeStruct((n, 64, VW), bf16),
             jax.ShapeDtypeStruct((n, 64, 2 * VW), f32),
-            jax.ShapeDtypeStruct((n, 64, 2 * VW), f32),
+            jax.ShapeDtypeStruct((n, 64, 2 * VW), bf16),
             jax.ShapeDtypeStruct((8, VW), f32),
         ],
-        in_specs=[SMEM, SMEM, SMEM] + [VMEM] * 7,
+        in_specs=[SMEM] + [VMEM] * 6 + [SMEM, VMEM],
         out_specs=[VMEM] * 4,
         scratch_shapes=[pltpu.VMEM((2 * rows, VW), f32)] * 2,
         compiler_params=pltpu.CompilerParams(vmem_limit_bytes=vmem_cap),
-        cost_estimate=pl.CostEstimate(
-            flops=30 * rows * rows * VW, bytes_accessed=30 * rows * VW, transcendentals=0
-        ),
-    )(order, core, lam, grad, *saved, gain)
-
-
-def to_heads(rows):
-    return rows.reshape(2, 2, 32, H, VW).transpose(3, 1, 0, 2, 4).reshape(H, 2, 64, VW)
-
-
-def from_heads(blocks):
-    lead = blocks.shape[:-4]
-    k = len(lead)
-    split = blocks.reshape(lead + (H, 2, 2, 32, VW))
-    order = tuple(range(k)) + (k + 2, k + 1, k + 3, k, k + 4)
-    return split.transpose(order).reshape(lead + (128, HW))
+        cost_estimate=busy(35),
+    )(lam, grad, *saved, gain)
+
+
+def swap_halves(rows):
+    count, width = rows.shape
+    return rows.reshape(2, 2, count // 4, width).transpose(1, 0, 2, 3).reshape(count, width)
 
 
 def body(
@@ -666,34 +851,29 @@
 ):
     n, tp, seq = place.n, place.tp, place.seq
     s, t, core, head, active = place.me()
-    lin = s * tp + t
+    inputs, cotangent = swap_halves(inputs), swap_halves(cotangent)
     row_count, width = inputs.shape
+    half = row_count // 2
     part = width // n
     inputs_f = inputs.astype(f32)
     attn_scale = rms_scale(inputs_f)
     attn_normed = (inputs_f * attn_scale * attn_gain).astype(bf16)
-    group_rows = lax.all_gather(
-        jnp.concatenate([inputs, cotangent], axis=1), "tp", axis=0, tiled=True
-    )
-    inputs_all, cotangent_all = group_rows[:, :width], group_rows[:, width:]
+    rows_all = lax.all_gather(inputs, ("seq", "tp"), axis=0, tiled=False)
     first_exp = jnp.exp(jnp.sum(lambda_params[0] * lambda_params[1]))
     second_exp = jnp.exp(jnp.sum(lambda_params[2] * lambda_params[3]))
     lambda_value = first_exp - second_exp + lambda_init
     lam = lambda_value.reshape(1)
 
-    payload = jnp.concatenate(
-        [to_heads(dot(attn_normed, w).astype(bf16)) for w in (w_query, w_key, w_value)], axis=3
-    )
-    own, sib, pos = send_heads(place, payload, positions.reshape(1, row_count), 1)
-    blocks = pos.reshape(2 * n, 64)[:, 0] // 64
-    run = jnp.arange(2 * n, dtype=jnp.int32)
-    order = jnp.sum(jnp.where(blocks[None, :] == run[:, None], run[None, :], 0), axis=1)
-    core_1 = core.reshape(1).astype(jnp.int32)
+    weights = (w_query, w_key, w_value)
+    own, sib, pos, cotangent_all = send_heads(
+        place, attn_normed, weights, positions.reshape(1, row_count), cotangent, 1
+    )
+    cotangent_all = cotangent_all.reshape(tp * row_count, width)
     head_gain = (sub_gain * (1.0 - lambda_init)).reshape(1, VW)
-    mixed, *saved = attend(place, order, core_1, lam, own, sib, head_gain)
-    normed_all = lax.all_gather(attn_normed, ("seq", "tp"), axis=0, tiled=True)
-    mixed_all = from_heads(return_heads(place, mixed, 2)).reshape(tp * row_count, HW)
-
+    mixed, *saved = attend(place, pos.reshape(n, row_count), lam, own, sib, head_gain)
+    mixed_all = return_heads(place, mixed, 2).reshape(tp * row_count, HW)
+
+    inputs_all = lax.dynamic_slice_in_dim(rows_all, s * tp, tp, 0).reshape(tp * row_count, width)
     middle_all = inputs_all.astype(f32) + dot(mixed_all, w_out)
     scale_all = rms_scale(middle_all)
     ffn_rows = (middle_all * scale_all * ffn_gain).astype(bf16)
@@ -710,12 +890,45 @@
     ).astype(bf16)
     up_rows_grad = (hidden_grad * gate_act).astype(bf16)
     ffn_partial = dot_nt(gate_rows_grad, w_gate) + dot_nt(up_rows_grad, w_up)
-    (grad_parts,) = moves(
+    hidden_width = hidden.shape[1]
+    chunk = 256
+
+    def ffn_weights(given, made, rest):
+        cot, rows, hid, gate, up = given
+        (out,) = made
+        held, sem = rest
+
+        def copy(i):
+            at = pl.ds(pl.multiple_of(chunk * i, chunk), chunk)
+            return pltpu.make_async_copy(held.at[at], out.at[at], sem.at[i])
+
+        def step(i):
+            at = pl.ds(pl.multiple_of(chunk * i, chunk), chunk)
+            for k, (left, right) in enumerate(((cot, hid), (rows, gate), (rows, up))):
+                held[at, k * hidden_width : (k + 1) * hidden_width] = dot_tn(
+                    left[:, at], right[...]
+                ).astype(bf16)
+            copy(i).start()
+
+        loop(width // chunk, step)
+        loop(width // chunk, lambda i: copy(i).wait())
+
+    grad_parts, ffn_parts = moves(
         place,
         [Group(place, False)],
         [ffn_partial.astype(bf16).reshape(tp, row_count, width)],
         [(tp, row_count, width)],
         3,
+        30,
+        work=ffn_weights,
+        operands=[
+            (a, VMEM) for a in (cotangent_all, ffn_rows, hidden, gate_rows_grad, up_rows_grad)
+        ],
+        results=[(jax.ShapeDtypeStruct((width, 3 * hidden_width), bf16), ANY)],
+        scratch=[
+            pltpu.VMEM((width, 3 * hidden_width), bf16),
+            pltpu.SemaphoreType.DMA((width // chunk,)),
+        ],
     )
     own_partial = lax.dynamic_slice_in_dim(ffn_partial, t * row_count, row_count, 0)
     member = jnp.arange(tp)[:, None, None]
@@ -726,58 +939,55 @@
     middle_grad = cotangent.astype(f32) + rms_back(middle, ffn_scale, ffn_gain, ffn_in_grad)
     branch_grad = middle_grad.astype(bf16)
 
-    down_part = dot_tn(cotangent_all, hidden).astype(bf16)
-    gate_part = dot_tn(ffn_rows, gate_rows_grad).astype(bf16)
-    up_part = dot_tn(ffn_rows, up_rows_grad).astype(bf16)
-
     def scatter_rows(array):
         return lax.psum_scatter(array, "seq", scatter_dimension=0, tiled=True)
 
-    down_grad = scatter_rows(down_part).astype(f32).T
-    gate_grad = scatter_rows(gate_part).astype(f32)
-    up_grad = scatter_rows(up_part).astype(f32)
-
-    mixed_grad = to_heads(dot_nt(branch_grad, w_out).astype(bf16))
-    grad_heads, branch_all = moves(
+    ffn_grads = scatter_rows(ffn_parts)
+
+    mixed_grad = dot_nt(branch_grad, w_out).astype(bf16)
+
+    def head_block(x, h, c):
+        return x.at[
+            pl.ds(pl.multiple_of(half * c, half), half), pl.ds(pl.multiple_of(VW * h, VW), VW)
+        ]
+
+    def ffn_result(given, made, rest):
+        hid, weight = given
+        (out,) = made
+        for i in range(tp):
+            out[i] = dot(hid[i * row_count : (i + 1) * row_count, :], weight[...]).astype(bf16)
+
+    grad_heads, ffn_out = moves(
         place,
-        [Dispatch(place), Group(place, True)],
-        [mixed_grad, branch_grad],
-        [(n, 64, VW), (tp, row_count, width)],
+        [Dispatch(place, head_block)],
+        [mixed_grad],
+        [(n, half, VW)],
         4,
-    )
-    mixed_cols = lax.dynamic_index_in_dim(
-        mixed_all.reshape(tp * row_count, seq, tp, part), t, 2, keepdims=False
-    ).reshape(tp * row_count, seq * part)
-    out_part = dot_tn(mixed_cols, branch_all.reshape(tp * row_count, width)).astype(bf16)
-    out_grad = scatter_rows(out_part).astype(f32)
-
-    dq, dkv, dkv_sib, sums = attend_back(place, order, core_1, lam, grad_heads, saved, head_gain)
-    swap = [(i, i ^ 1) for i in range(seq)]
-    dkv = dkv + lax.ppermute(dkv_sib, "seq", swap)
-    back = jnp.concatenate([dq, dkv.astype(bf16)], axis=2)
-
-    ffn_out = dot(hidden, w_down)
-    rows_back, out_parts = moves(
+        20,
+        work=ffn_result,
+        operands=[(hidden, VMEM), (w_down, VMEM)],
+        results=[(jax.ShapeDtypeStruct((tp, row_count, width), bf16), VMEM)],
+    )
+    dq, dkv, dkv_sib, sums = attend_back(place, lam, grad_heads, saved, head_gain)
+    normed_grad, weight_half, out_parts, branch_all = finish_heads(
         place,
-        [Collect(place), Group(place, False)],
-        [back, ffn_out.astype(bf16).reshape(tp, row_count, width)],
-        [(H, 2, 64, 3 * VW), (tp, row_count, width)],
+        dq,
+        dkv,
+        dkv_sib,
+        rows_all,
+        attn_gain.reshape(1, width),
+        weights,
+        ffn_out,
+        branch_grad,
         5,
     )
+    out_part = dot_tn(mixed_all, branch_all.reshape(tp * row_count, width)).astype(bf16)
+    out_part = lax.dynamic_index_in_dim(
+        out_part.reshape(seq, tp, part, width), t, 1, keepdims=False
+    ).reshape(seq * part, width)
+    out_part, ffn_grads = lax.optimization_barrier((out_part, ffn_grads))
+
     output = (middle + jnp.sum(out_parts.astype(f32), axis=0)).astype(bf16)
-
-    normed_half = lax.dynamic_index_in_dim(
-        normed_all.reshape(n, 2, 2, 32, width), core, 2, keepdims=False
-    ).reshape(n * 64, width)
-    weight_part = dot_tn(normed_half, back.reshape(n * 64, 3 * VW))
-    keep = lax.dynamic_slice_in_dim(weight_part, core * (width // 2), width // 2, 0)
-    away = lax.dynamic_slice_in_dim(weight_part, (1 - core) * (width // 2), width // 2, 0)
-    weight_half = (keep + lax.ppermute(away, "seq", swap)).astype(bf16)
-
-    normed_grad = sum(
-        dot_nt(from_heads(rows_back[..., i * VW : (i + 1) * VW]), w)
-        for i, w in enumerate((w_query, w_key, w_value))
-    )
     attn_gain_part = jnp.sum(normed_grad * inputs_f * attn_scale, axis=0)
     input_grad = middle_grad + rms_back(inputs_f, attn_scale, attn_gain, normed_grad)
 
@@ -793,13 +1003,20 @@
         + [jnp.zeros((n, VW), f32)] * 4,
         axis=1,
     )
+    small, out_part = lax.optimization_barrier((small, out_part))
     weight_rows, small_all = moves(
         place,
-        [Collect(place, True), Everyone(place, False)],
+        [Collect(place, lambda o, t, h, c: o.at[h], True), Everyone(place, False)],
         [weight_half.reshape(n // 2, part, 3 * VW), small],
         [(H, part, 3 * VW), (n, 8, VW)],
         6,
-    )
+        20,
+    )
+    out_grad = scatter_rows(out_part).astype(f32)
+    ffn_grads = ffn_grads.astype(f32)
+    down_grad = ffn_grads[:, :hidden_width].T
+    gate_grad = ffn_grads[:, hidden_width : 2 * hidden_width]
+    up_grad = ffn_grads[:, 2 * hidden_width :]
     weight_rows = weight_rows.astype(f32).reshape(H, part, 3, VW).transpose(2, 1, 0, 3)
     weight_rows = weight_rows.reshape(3, part, HW)
     small_sum = jnp.sum(small_all, axis=0)
@@ -813,6 +1030,7 @@
         ]
     )
     lambda_norm = jnp.sqrt(jnp.sum(lambda_grads * lambda_grads))
+    output, input_grad = swap_halves(output), swap_halves(input_grad)
     return (
         output,
         input_grad,

time: 528 us -> 418 us (0.79); the launches traced: 517 us -> 417 us
  local copies, waits for them, and re-layouts: 74.5 us -> 25.2 us
  matrix products: 75.5 us -> 31 us
  Pallas kernels: 281 us -> 321 us
  waiting for transfers between devices: 29.2 us -> 0.07 us
  other arithmetic: 37 us -> 20.3 us
    pallas_call x2 -> x3, Pallas kernels: 86.3 us -> 154 us  [the longest x1 67.3 us: finish_heads(): pl.pallas_call(kernel, out_shape=[jax.ShapeDtypeStruct((2 * half, width),...]
    pallas_call x4 -> x3, Pallas kernels: 126 us -> 96.6 us  [moves(): pl.pallas_call(kernel, out_shape=[jax.ShapeDtypeStruct(s, a.dtype) for s,...]
    reduce_scatter x4 -> x2, waiting for transfers between devices: 29.1 us -> 0.01 us  [scatter_rows(): return lax.psum_scatter(array, 'seq', scatter_dimension=0, tiled=True)]
    dot_general x7 -> x3, matrix products: 29.3 us -> 10.1 us  [dot(): return jnp.dot(left, right, preferred_element_type=f32)]
    dot_general x5 -> x1, matrix products: 22.5 us -> 4.53 us  [dot_tn(): lax.dot_general(left, right, (((0,), (0,)), ((), ())), preferred_element_...]
    dynamic_slice x4 -> x2, local copies, waits for them, and re-layouts: 16.5 us -> 2.79 us  [the longest x1 1.63 us: body(): lax.dynamic_slice_in_dim(rows_all, s * tp, tp, 0)]
    reshape x9 -> x2, local copies, waits for them, and re-layouts: 14.3 us -> 3.68 us  [swap_halves(): rows.reshape(2, 2, count // 4, width).transpose(1, 0, 2, 3)]
    another operation x1 -> x0, local copies, waits for them, and re-layouts: 9.61 us -> none  [body(): mixed_all.reshape(tp * row_count, seq, tp, part)]
  transfers between devices with their start and end apart: 8 -> 3, of which waited for: 1 -> 0; matrix products, arithmetic and copies ran while one was open for 32% -> 12% of each run, Pallas kernels for 50% -> 68%
where the time goes in v2:
time: 418 us; the launch traced here: 417 us
  Pallas kernels  321 us (77%)
  matrix products  31 us (7%)
  local copies, waits for them, and re-layouts  25.2 us (6%)
  other arithmetic  20.3 us (5%)
  between operations  18.7 us (4%)
    pallas_call x3, Pallas kernels, moves(): pl.pallas_call(kernel, out_shape=[jax.ShapeDtypeStruct(s, a.dtype) for s,...  96.6 us
    pallas_call x1, Pallas kernels, finish_heads(): pl.pallas_call(kernel, out_shape=[jax.ShapeDtypeStruct((2 * half, width),...  67.3 us
    pallas_call x1, Pallas kernels, send_heads(): pl.pallas_call(kernel, grid=(H,), out_shape=[jax.ShapeDtypeStruct((n, row...  52.1 us
    pallas_call x1, Pallas kernels, attend_back(): pl.pallas_call(functools.partial(bwd_kernel, n), out_shape=[jax.ShapeDtyp...  36.4 us
    pallas_call x1, Pallas kernels, return_heads(): pl.pallas_call(kernel, out_shape=jax.ShapeDtypeStruct((place.tp, 2 * rows...  34.5 us
    pallas_call x1, Pallas kernels, attend(): pl.pallas_call(functools.partial(fwd_kernel, n), out_shape=[jax.ShapeDtyp...  34.1 us
    dot_general x4, matrix products, dot_nt(): lax.dot_general(left, right, (((1,), (1,)), ((), ())), preferred_element_...  16.4 us
    dot_general x3, matrix products, dot(): return jnp.dot(left, right, preferred_element_type=f32)  10.1 us
  transfers between devices with their start and end apart: 3, of which 0 were waited for; matrix products, arithmetic and copies ran while one was open for 12% of the time, Pallas kernels for 68%

profile of v2, /device:TPU:0, one launch (start us, length us, event | category | flops | bytes accessed | tf_op | source)
XLA Modules:
  0.0 416.6 jit_solution(14890852767314291679)
XLA Ops:
  7.3 1.9 copy.45
  9.3 1.1 fusion.1
  10.4 0.6 rsqrt.34
  11.0 1.8 copy.46
  12.8 0.6 multiply_reduce_fusion.5
  14.8 1.6 fusion.3.x
  16.4 1.2 multiply_bitcast_fusion.gain
  17.6 52.1 %shard_map.253 = (bf16[32,64,384]{2,1,0:T(8,128)(2,1)}, bf16[32,64,256]{2,1,0:T(8,128)(2,1)}, s32[32,1,128]{2,1,0:T(1,128)}, bf16[4,128,1536]{2,1,0:T(8,128)(2,1)}) custom-call(bf16[128,1536]{1,0:T(8,128)(2,1)} %fusion.3.x, bf16[1536,1536]{1,0:T(8,128)(2,1)} %refs_5_.1, bf16[1536,1536]{1,0:T(8,128)(2,1)} %refs_6_.1, bf16[1536,1536]{1,0:T(8,128)(2,1)} %refs_7_.1, ...), custom_call_target="tpu_custom_call" | custom-call | flops 35000000512 | bytes 105000000 | tf_op jit(solution)/shard_map/pallas_call | solution.py:402
  69.7 5.5 %fusion.14 = f32[512,1024]{1,0:T(8,128)} fusion(bf16[512,1536]{1,0:T(8,128)(2,1)} %bitcast.129, bf16[1024,1536]{1,0:T(8,128)(2,1)} %refs_2_.1), kind=kOutput, calls=%fused_computation.67 | convolution fusion | flops 1610612736 | bytes 6815744 | tf_op jit(solution)/shard_map/dot_general | solution.py:37
  75.2 34.1 %shard_map.254 = (bf16[32,64,128]{2,1,0:T(8,128)(2,1)}, f32[2,2048,128]{2,1,0:T(8,128)}, f32[8,8,512]{2,1,0:T(8,128)}, bf16[2048,128]{1,0:T(8,128)(2,1)}, bf16[4...) custom-call(s32[32,128]{1,0:T(8,128)} %bitcast.133, f32[1]{0:T(128)} %bitcast.10.lam, ...), custom_call_target="tpu_custom_call" | custom-call | flops 30000001024 | bytes 90000000 | tf_op jit(solution)/shard_map/pallas_call | solution.py:691
  109.3 34.5 %shard_map.255 = bf16[4,128,1536]{2,1,0:T(8,128)(2,1)} custom-call(bf16[32,64,128]{2,1,0:T(8,128)(2,1)} %get-tuple-element.47.x), custom_call_target="tpu_custom_call" | custom-call | flops 35000000512 | bytes 105000000 | tf_op jit(solution)/shard_map/pallas_call | solution.py:461
  143.9 1.6 constant_dynamic-slice_fusion.1
  145.5 0.2 copy-done.25
  145.7 4.6 %multiply_reduce_fusion = (f32[512]{0:T(512)S(1)}, f32[512,1536]{1,0:T(8,128)S(1)}) fusion(bf16[512,1536]{1,0:T(8,128)(2,1)S(1)} %bitcast.128, bf16[1536,1536]{1,0:T(8,128)(2,1)} %param.20, bf16[512,1536]{1,0:T(8,128)(2,1)S(1)} %bitcast.116), kind=kOutput, calls=%fused_computation.6 | convolution fusion | flops 2419064320 | bytes 11012096 | tf_op jit(solution)/shard_map/dot_general | solution.py:29
  150.4 0.3 multiply_convert_fusion.refs_2_
  150.8 1.3 copy-done.2
  152.0 1.4 copy-done.24
  153.4 1.9 fusion.15
  155.3 0.3 copy-done.27
  155.6 3.6 multiply_convert_fusion.1
  159.2 1.8 fusion.16
  161.1 4.1 fusion.13
  165.2 38.9 %shard_map.256 = (bf16[4,128,1536]{2,1,0:T(8,128)(2,1)}, bf16[1536,3072]{1,0:T(8,128)(2,1)}) custom-call(bf16[4,128,1536]{2,1,0:T(8,128)(2,1)} %bitcast.131, bf16[512,1536]{1,0:T(8,128)(2,1)} %bitcast.130, bf16[512,1536]{1,0:T(8,128)(2,1)} %copy-done.10, bf16[512,1024]{1,0:T(8,128)(2,1)} %get-tuple-element.83.refs_3_.refs_1_, bf16[512,1024]{1,0:T(8,128)(2,1)} %copy-done.28, ...), custom_call_target="tpu_custom_call" | custom-call | flops 30000001024 | bytes 90000000 | tf_op jit(solution)/shard_map/pallas_call | solution.py:332
  204.1 0.3 reduce-scatter.5.cloned.1.call-start
  204.4 0.4 copy-done.15
  204.7 0.6 broadcast_in_dim.30.refs_4_
  205.3 0.5 multiply_multiply_fusion
  205.9 0.1 copy-done.3
  206.0 0.1 multiply_reduce_fusion.3
  206.1 2.1 select_reduce_fusion
  208.2 0.3 multiply_reduce_fusion.1
  208.5 1.2 fusion.10
  209.7 4.9 %convolution_convert_fusion.refs_0_ = bf16[128,1536]{1,0:T(8,128)(2,1)} fusion(bf16[128,1536]{1,0:T(8,128)(2,1)S(1)} %get-tuple-element.81.refs_9_, bf16[1536,1536]{1,0:T(8,128)(2,1)} %param.20), kind=kOutput, calls=%fused_computation.7 | convolution fusion | flops 604176384 | bytes 5505024 | tf_op jit(solution)/shard_map/dot_general | solution.py:37
  214.6 24.0 %shard_map.257 = (bf16[32,64,128]{2,1,0:T(8,128)(2,1)}, bf16[4,128,1536]{2,1,0:T(8,128)(2,1)}) custom-call(bf16[128,1536]{1,0:T(8,128)(2,1)} %convolution_convert_fusion.refs_0_, bf16[512,1024]{1,0:T(8,128)(2,1)} %get-tuple-element.83.refs_3_.refs_1_, bf16[1024,1536]{1,0:T(8,128)(2,1)} %refs_2_.1), custom_call_target="tpu_custom_call" | custom-call | flops 20000000000 | bytes 60000000 | tf_op jit(solution)/shard_map/pallas_call | solution.py:332
  238.6 36.4 %shard_map.258 = (bf16[32,64,128]{2,1,0:T(8,128)(2,1)}, f32[32,64,256]{2,1,0:T(8,128)}, bf16[32,64,256]{2,1,0:T(8,128)(2,1)}, f32[8,128]{1,0:T(8,128)}) custom-call(f32[1]{0:T(128)} %bitcast.10.lam, bf16[32,64,128]{2,1,0:T(8,128)(2,1)} %get-tuple-element.50.grad, f32[2,2048,128]{2,1,0:T(8,128)} %get-tuple-element.51.mix, ...), custom_call_target="tpu_custom_call" | custom-call | flops 35000000512 | bytes 105000000 | tf_op jit(solution)/shard_map/pallas_call | solution.py:814
  275.0 67.3 %shard_map.259 = (f32[128,1536]{1,0:T(8,128)}, bf16[768,384]{1,0:T(8,128)(2,1)}, bf16[4,128,1536]{2,1,0:T(8,128)(2,1)}, bf16[4,128,1536]{2,1,0:T(8,128)(2,1)}) custom-call(bf16[32,64,128]{2,1,0:T(8,128)(2,1)} %get-tuple-element.57.refs_0_, f32[32,64,256]{2,1,0:T(8,128)} %get-tuple-element.58.refs_1_, bf16[32,64,256]{2,1,0:T(8,128)(2,1)} %get-tuple-element.59.refs_2_, ...), custom_call_target="tpu_custom_call" | custom-call | flops 40000000000 | bytes 120000000 | tf_op jit(solution)/shard_map/pallas_call | solution.py:569
  342.3 2.0 fusion.9
  344.3 1.4 reshape.186
  345.6 0.7 reshape.187
  346.3 1.4 pad.7
  347.8 1.3 pad.8
  349.1 0.7 broadcast_multiply_fusion
  349.7 1.7 fusion.6
  351.4 0.9 copy.48
  352.4 0.2 convert_reduce_fusion
  352.6 0.1 add_convert_fusion
  352.7 0.8 copy.47
  353.6 0.8 stack.22.refs_1_
  354.4 4.5 %bitcast_convert_fusion = bf16[1536,1536]{1,0:T(8,128)(2,1)S(1)} fusion(bf16[4,128,1536]{2,1,0:T(8,128)(2,1)} %shard_map.255, bf16[4,128,1536]{2,1,0:T(8,128)(2,1)} %get-tuple-element.65), kind=kOutput, calls=%fused_computation | convolution fusion | flops 2418278400 | bytes 7864320 | tf_op jit(solution)/shard_map/dot_general | solution.py:33
  358.9 1.2 constant_dynamic-slice_fusion
  360.1 33.7 %shard_map.260 = (bf16[12,48,384]{2,1,0:T(8,128)(2,1)}, f32[32,8,128]{2,1,0:T(8,128)}) custom-call(bf16[16,48,384]{2,1,0:T(8,128)(2,1)} %bitcast.132, f32[32,8,128]{2,1,0:T(8,128)} %stack.22.refs_1_), custom_call_target="tpu_custom_call" | custom-call | flops 20000000000 | bytes 60000000 | tf_op jit(solution)/shard_map/pallas_call | solution.py:332
  393.8 1.0 reduce_sum.137
  394.8 1.1 slice_bitcast_fusion.2
  397.3 1.7 convert_element_type.83
  398.9 1.2 multiply_reduce_fusion.4
  400.8 0.3 reshape.193
  401.2 0.6 fusion.12
  401.8 0.1 copy.51
  401.9 0.1 copy.52
  402.1 0.8 copy.65
  402.9 0.5 slice_bitcast_fusion.1
  403.5 2.9 fusion.11
  406.3 1.0 copy_bitcast_fusion
  407.3 1.6 convert_element_type.82
  (72 shorter events, 0.5 us)
Async XLA Ops:
  7.2 148.1 %copy-start = (bf16[1536,1024]{1,0:T(8,128)(2,1)S(1)}, bf16[1536,1024]{1,0:T(8,128)(2,1)}, u32[]{:S(2)}) copy-start(bf16[1536,1024]{1,0:T(8,128)(2,1)} %param.25) | copy-start | bytes 9437188
  7.2 7.6 %copy-start.4 = (bf16[128,1536]{1,0:T(8,128)(2,1)S(1)}, bf16[128,1536]{1,0:T(8,128)(2,1)}, u32[]{:S(2)}) copy-start(bf16[128,1536]{1,0:T(8,128)(2,1)} %param.14) | copy-start | bytes 1179652
  7.2 5.6 %copy-start.19 = (f32[4,64]{1,0:T(4,128)S(1)}, f32[4,64]{1,0:T(4,128)}, u32[]{:S(2)}) copy-start(f32[4,64]{1,0:T(4,128)} %param.21) | copy-start | bytes 3076
  7.2 7.6 %copy-start.14 = (f32[1536]{0:T(1024)S(1)}, f32[1536]{0:T(1024)}, u32[]{:S(2)}) copy-start(f32[1536]{0:T(1024)} %param.16) | copy-start | bytes 18436
  7.2 136.6 %all-gather.2.cloned.1.call-start = ((), (), s32[]{:S(2)}) async-start(), calls=%async_computation.2 | async-start | bytes 12976128 | tf_op jit(solution)/shard_map/all_gather | solution.py:861
  9.2 350.8 %reduce-scatter.3.cloned.1.call-start = ((), (), s32[]{:S(2)}) async-start(), calls=%async_computation.3 | async-start | bytes 10616832 | tf_op jit(solution)/shard_map/reduce_scatter | solution.py:943
  143.8 1.9 copy-start.25
  145.7 4.7 %copy-start.16 = (f32[1536]{0:T(1024)S(1)}, f32[1536]{0:T(1024)}, u32[]{:S(2)}) copy-start(f32[1536]{0:T(1024)} %param.23) | copy-start | bytes 18436
  150.4 1.7 copy-start.2
  150.4 3.0 copy-start.24
  153.4 1.9 copy-start.10
  153.4 2.2 copy-start.27
  159.2 1.8 copy-start.28
  159.2 1.9 copy-start.26
  204.0 0.7 copy-start.15
  204.1 1.3 copy-start.21
  204.1 1.9 copy-start.3
  204.1 203.2 %reduce-scatter.5.cloned.1.call-start = ((), (), s32[]{:S(2)}) async-start(), calls=%async_computation.4 | async-start | bytes 1327104 | tf_op jit(solution)/shard_map/reduce_scatter | solution.py:943
  205.3 2.9 copy-start.12
  206.1 2.4 copy-start.9
  209.7 4.9 %copy-start.11 = (bf16[128,1536]{1,0:T(8,128)(2,1)}, bf16[128,1536]{1,0:T(8,128)(2,1)S(1)}, u32[]{:S(2)}) copy-start(bf16[128,1536]{1,0:T(8,128)(2,1)S(1)} %get-tuple-element.81.refs_9_) | copy-start | bytes 1179652
  275.0 67.3 %copy-start.5 = (bf16[128,1536]{1,0:T(8,128)(2,1)S(1)}, bf16[128,1536]{1,0:T(8,128)(2,1)}, u32[]{:S(2)}) copy-start(bf16[128,1536]{1,0:T(8,128)(2,1)} %param.14) | copy-start | bytes 1179652
  275.0 67.3 %copy-start.22 = (f32[128]{0:T(128)S(1)}, f32[128]{0:T(128)}, u32[]{:S(2)}) copy-start(f32[128]{0:T(128)} %rsqrt.34) | copy-start | bytes 1540
  346.3 6.1 %copy-start.8 = (bf16[4,128,1536]{2,1,0:T(8,128)(2,1)S(1)}, bf16[4,128,1536]{2,1,0:T(8,128)(2,1)}, u32[]{:S(2)}) copy-start(bf16[4,128,1536]{2,1,0:T(8,128)(2,1)} %get-tuple-element.61) | copy-start | bytes 4718596
  352.4 1.1 copy-start.23
  352.4 1.2 copy-start.17
  352.4 1.2 copy-start.18
  360.1 37.2 %copy-start.6 = (bf16[192,3072]{1,0:T(8,128)(2,1)S(1)}, bf16[192,3072]{1,0:T(8,128)(2,1)}, u32[]{:S(2)}) copy-start(bf16[192,3072]{1,0:T(8,128)(2,1)} %reduce-scatter.3.cloned.1.call-done) | copy-start | bytes 3538948
  393.8 5.1 %copy-start.20 = (f32[4,64]{1,0:T(4,128)S(1)}, f32[4,64]{1,0:T(4,128)}, u32[]{:S(2)}) copy-start(f32[4,64]{1,0:T(4,128)} %param.21) | copy-start | bytes 3076
  393.8 7.0 %copy-start.13 = (bf16[12,48,384]{2,1,0:T(8,128)(2,1)S(1)}, bf16[12,48,384]{2,1,0:T(8,128)(2,1)}, u32[]{:S(2)}) copy-start(bf16[12,48,384]{2,1,0:T(8,128)(2,1)} %get-tuple-element.70) | copy-start | bytes 1327108
  401.2 2.3 copy-start.7
  402.9 6.0 %copy-start.1 = (bf16[1536,1024]{1,0:T(8,128)(2,1)S(1)}, bf16[1536,1024]{1,0:T(8,128)(2,1)}, u32[]{:S(2)}) copy-start(bf16[1536,1024]{1,0:T(8,128)(2,1)} %param.25) | copy-start | bytes 9437188
Sparse Core Ops, SparseCore 0:
  11.5 130.5 all-gather.1
  204.2 125.7 reduce-scatter.2
  360.2 38.6 reduce-scatter.4
